TPU v7x, 32 devices: a whole 2x2x4 slice. The times are simulated.
32 devices in a mesh: groups: 2 (over y), loop: 4 (over z), enc: 2 (over x), rep: 2 (over core).
Axes of the slice: x: 2, y: 2, z: 4, core: 2. Of those that a mesh axis runs over, the one named last changes fastest.
Arguments:
- embeddings: bfloat16 [4096, 768], P(('groups', 'loop', 'rep'), 'enc'), parts along dimension 0, may hold values from -24 to 24
- head_weight: bfloat16 [768, 768], P('enc'), may hold values from -0.21875 to 0.21875
- gp_weights: float32 [4096], P('groups'), parts along dimension 0, may hold values from -24 to 24
- counts: int32 [8], P('groups'), parts along dimension 0, may hold values from 64 to 512, as said below
Outputs:
- embed_grad: bfloat16 [4096, 768], P(('groups', 'loop', 'rep'), 'enc'), parts along dimension 0
- head_grad: float32 [1536, 768], P(('groups', 'enc')), parts along dimension 0
There are 2 independent parts, one for each index of `groups`. A program takes and returns all parts, laid end to end along the dimension named above; an argument that names none is the same for every part. Nothing has to cross between parts.
Inputs may be any that keep to these rules, and one draw needn't show every extreme that they name: `counts`: some block is full and some block holds exactly 64 valid molecules.
All inputs are finite; a program needn't handle non-finite values.
Results may differ from a plain program's by a relative error of at most 0.019.
Values may be sent and summed in bfloat16 or wider, within the bound.
No kernel may reach another device: no remote copies, remote signals or barrier semaphores. Data moves between devices by JAX's collectives and lax.ppermute only.
A program may use at most 64 MiB of HBM per device.

v0:
```python
import jax
import jax.numpy as jnp
from jax import lax
from jax.experimental import pallas as pl
from jax.experimental.pallas import tpu as pltpu
from jax.sharding import PartitionSpec as P

EPSILON = 1e-06
TILE = 128
CHUNK = 2 * TILE


def passed_along(value, axis, steps):
    count = lax.axis_size(axis)
    pairs = [(source, (source + steps) % count) for source in range(count)]
    return lax.ppermute(value, axis, pairs)


def ring_body(embeddings, head_weight, gp_weights, counts):
    enc_size = lax.axis_size("enc")
    rep_size = lax.axis_size("rep")
    loop_size = lax.axis_size("loop")
    share_rows = embeddings.shape[0]
    piece_rows = share_rows // enc_size
    block_rows = share_rows * rep_size
    loop_index = lax.axis_index("loop")
    enc_index = lax.axis_index("enc")
    rep_index = lax.axis_index("rep")
    own_feats = lax.psum_scatter(
        jnp.dot(embeddings, head_weight, preferred_element_type=jnp.float32),
        "enc",
        scatter_dimension=0,
        tiled=True,
    ).astype(jnp.bfloat16)
    block_feats = lax.all_gather(own_feats, ("enc", "rep"), axis=0, tiled=True)
    block_norms = jnp.sum(jnp.square(block_feats.astype(jnp.float32)), axis=1)
    offsets = (
        jnp.arange(rep_size, dtype=jnp.int32)[None, :, None] * share_rows
        + jnp.arange(enc_size, dtype=jnp.int32)[:, None, None] * piece_rows
        + jnp.arange(piece_rows, dtype=jnp.int32)[None, None, :]
    ).reshape(block_rows)
    own_base = lax.dynamic_slice_in_dim(gp_weights, loop_index * block_rows, block_rows)
    block_coef = (
        own_base.reshape(rep_size, enc_size, piece_rows).transpose(1, 0, 2).reshape(block_rows)
    )
    own_count = lax.dynamic_index_in_dim(counts, loop_index, keepdims=False)
    block_coef = jnp.where(offsets < own_count, block_coef, 0.0)
    piece_start = rep_index * share_rows + enc_index * piece_rows
    piece_offsets = piece_start + jnp.arange(piece_rows, dtype=jnp.int32)

    def tile(state, piece, anchor):
        anchor_count = lax.dynamic_index_in_dim(counts, anchor, keepdims=False)
        accum, quotient_sum = state
        piece_coef = lax.dynamic_slice_in_dim(
            gp_weights, anchor * block_rows + piece_start, piece_rows
        )
        piece_coef = jnp.where(piece_offsets < anchor_count, piece_coef, 0.0)
        piece_norms = jnp.sum(jnp.square(piece.astype(jnp.float32)), axis=1)
        scores = lax.dot_general(
            piece, block_feats, (((1,), (1,)), ((), ())), preferred_element_type=jnp.float32
        )
        denom = piece_norms[:, None] + block_norms[None, :] - scores + EPSILON
        inverse = 1.0 / (denom * denom)
        pair_coef = piece_coef[:, None] * block_coef[None, :]
        pair_weight = (pair_coef * (piece_norms[:, None] + block_norms[None, :]) * inverse).astype(
            jnp.bfloat16
        )
        quotient_sum = quotient_sum + jnp.sum(pair_coef * 2.0 * scores * inverse, axis=0)
        accum = accum + lax.dot_general(
            pair_weight, piece, (((0,), (0,)), ((), ())), preferred_element_type=jnp.float32
        )
        return (accum, quotient_sum)

    start_state = (
        jnp.zeros((block_rows, block_feats.shape[1]), jnp.float32),
        jnp.zeros((block_rows,), jnp.float32),
    )
    state = tile(start_state, own_feats, loop_index)

    def forward_step(step_index, carry):
        moving, inner = carry
        moving = passed_along(moving, "loop", 1)
        inner = tile(inner, moving, (loop_index - step_index - 1 + loop_size) % loop_size)
        return (moving, inner)

    moving, state = lax.fori_loop(0, loop_size - 1, forward_step, (own_feats, state))
    accum, quotient_sum = state
    grad_block = accum - block_feats.astype(jnp.float32) * quotient_sum[:, None]
    own_grad = lax.psum_scatter(
        grad_block.astype(jnp.bfloat16), ("enc", "rep"), scatter_dimension=0, tiled=True
    )
    piece = lax.all_gather(own_grad, "enc", axis=0, tiled=True)
    embed_part = lax.dot_general(
        piece, head_weight, (((1,), (1,)), ((), ())), preferred_element_type=jnp.float32
    )
    head_part = lax.dot_general(
        embeddings, piece, (((0,), (0,)), ((), ())), preferred_element_type=jnp.float32
    )
    head_grad = lax.psum(head_part, ("loop", "rep"))
    return (embed_part.astype(jnp.bfloat16), head_grad)


OWN_ORDER = ((0, 0), (0, 1), (2, 0), (2, 1), (3, 1), (3, 0), (1, 1), (1, 0))
SLOTS = [(0, k, h) for k, h in OWN_ORDER] + [(1, k, h) for k, h in OWN_ORDER[::-1]]
LENT = ((1, 0), (1, 1), (3, 0), (3, 1))
PLACES = 24


def turned(row):
    return jnp.transpose(jnp.broadcast_to(row, (TILE, TILE)))[:, :1]


def prep_kernel(counts_ref, gp_ref, weights, places):
    z = lax.axis_index("loop")
    rep = lax.axis_index("rep")
    lane = lax.broadcasted_iota(jnp.int32, (1, TILE), 1)
    weights[...] = jnp.zeros_like(weights)
    total = jnp.int32(0)
    totals = []
    for slot, (other, k, h) in enumerate(SLOTS):
        block = jnp.bitwise_xor(z, k)
        piece = rep if other == 0 else 1 - rep
        base = piece * (2 * TILE) + h * TILE
        count = counts_ref[block]
        valid = count > base

        @pl.when(valid)
        def _(block=block, piece=piece, h=h, base=base, count=count, total=total):
            row = gp_ref[pl.ds(block * 4 + piece * 2 + h, 1), :]
            weights[pl.ds(total, 1), :] = jnp.where(lane + base < count, row, 0.0)

        places[slot] = jnp.where(valid, total, -1)
        total = total + valid.astype(jnp.int32)
        totals.append(total)
    own = totals[len(OWN_ORDER) - 1]
    places[16] = total
    places[17] = jnp.where(rep == 0, (total + 1) // 2, total // 2)
    places[18] = jnp.clip(counts_ref[z] - rep * (2 * TILE), 0, 2 * TILE)
    places[19] = own


def tile_at(place):
    return pl.ds(pl.multiple_of(place * TILE, TILE), TILE)


def pack_tiles(places, pieces, rows_of, feats, norms, near):
    width = feats.shape[1]
    for slot, (other, k, h) in enumerate(SLOTS):
        if (other, k) not in pieces:
            continue
        place = places[slot]

        @pl.when(place >= 0)
        def _(place=place, other=other, k=k, h=h):
            here = slice(h * TILE, (h + 1) * TILE)
            value = pieces[other, k][here, :]
            feats[tile_at(place), :] = value
            wide = value.astype(jnp.float32)
            square = wide * wide
            part = square[:, :TILE]
            for s in range(1, width // TILE):
                part += square[:, s * TILE : (s + 1) * TILE]
            norms[pl.ds(place, 1), :] = jnp.sum(jnp.transpose(part), axis=0, keepdims=True)
            if (other, k) in rows_of:
                near[tile_at(place), :] = rows_of[other, k][here, :]


def pack_kernel(
    places,
    near0,
    near1,
    near2,
    near3,
    lent1,
    own0,
    own1,
    own2,
    own3,
    other0,
    other1,
    feats,
    norms,
    near,
):
    pieces = {
        (0, 0): own0,
        (0, 1): own1,
        (0, 2): own2,
        (0, 3): own3,
        (1, 0): other0,
        (1, 1): other1,
    }
    rows_of = {(0, 0): near0, (0, 1): near1, (0, 2): near2, (0, 3): near3, (1, 1): lent1}
    pack_tiles(places, pieces, rows_of, feats, norms, near)


def pair_kernel(
    places,
    weights,
    lent3,
    other2,
    other3,
    feats_in,
    norms_in,
    near_in,
    feats,
    norms,
    near,
    own_out,
    head_out,
    head_sent,
    grads,
):
    del feats_in, norms_in, near_in
    width = feats.shape[1]
    total, rows_here, own_valid = places[16], places[17], places[18]
    pack_tiles(
        places, {(1, 2): other2, (1, 3): other3}, {(1, 3): lent3}, feats, norms, near
    )
    feats[tile_at(total), :] = jnp.zeros((TILE, width), jnp.bfloat16)
    norms[pl.ds(total, 1), :] = jnp.zeros((1, TILE), jnp.float32)

    def row_chunk(i, deep, tiles):
        size = deep * TILE
        rows = pl.ds(pl.multiple_of(i * size, TILE), size)
        left = feats[rows, :]
        right = feats[: tiles * TILE, :]
        places_of = [pl.ds(deep * i + t, 1) for t in range(deep)]
        left_norms = jnp.concatenate([turned(norms[at, :]) for at in places_of], axis=0)
        coef = jnp.concatenate([turned(weights[at, :]) for at in places_of], axis=0)
        scores = lax.dot_general(
            left, right, (((1,), (1,)), ((), ())), preferred_element_type=jnp.float32
        )
        all_norms = jnp.concatenate([norms[t : t + 1, :] for t in range(tiles)], axis=1)
        all_coef = jnp.concatenate([weights[t : t + 1, :] for t in range(tiles)], axis=1)
        both = left_norms + all_norms
        denom = both - scores + EPSILON
        scaled = all_coef * (1.0 / (denom * denom))
        pair = (scaled * both).astype(jnp.bfloat16)
        quotient = 2.0 * jnp.sum(scaled * scores, axis=1, keepdims=True)
        carried = jnp.dot(pair, right, preferred_element_type=jnp.float32)
        row = lax.broadcasted_iota(jnp.int32, (size, 1), 0) + i * size
        coef = jnp.where(row < rows_here * TILE, coef, 0.0)
        grad = coef * (carried - left.astype(jnp.float32) * quotient)
        grads[rows, :] = grad.astype(jnp.bfloat16)

    row_tiles = jnp.maximum(2 * ((rows_here + 1) // 2), 4)

    @pl.when(row_tiles > rows_here)
    def _():
        near[tile_at(row_tiles - 1), :] = jnp.zeros((TILE, near.shape[1]), near.dtype)

    col_tiles = jnp.maximum(2 * ((total + 1) // 2), 8)
    for count, deep, columns in ((4, 2, (8, 10)), (6, 3, (10, 12, 14)), (8, 2, (14,))):
        for tiles in columns:

            @pl.when(jnp.logical_and(col_tiles == tiles, row_tiles == count))
            def _(count=count, deep=deep, tiles=tiles):
                def step(i, _):
                    row_chunk(i, deep, tiles)
                    return 0

                lax.fori_loop(0, count // deep, step, 0)

        @pl.when(row_tiles == count)
        def _(count=count):
            rows = slice(0, count * TILE)
            head = lax.dot_general(
                near[rows, :],
                grads[rows, :],
                (((0,), (0,)), ((), ())),
                preferred_element_type=jnp.float32,
            )
            head_out[...] = head
            head_sent[...] = head.astype(jnp.bfloat16)

    own = grads[:CHUNK, :]
    row = lax.broadcasted_iota(jnp.int32, (CHUNK, 1), 0)
    own_out[...] = jnp.where(row < own_valid, own, jnp.zeros_like(own))


def gathered_body(embeddings, head_weight, gp_weights, counts):
    loop_size = lax.axis_size("loop")
    rep = lax.axis_index("rep")
    share_rows, share_cols = embeddings.shape
    enc_rows, width = head_weight.shape

    def across_z(value, step):
        return lax.ppermute(value, "loop", [(i, i ^ step) for i in range(loop_size)])

    def across_x(value):
        return lax.ppermute(value, "enc", [(0, 1), (1, 0)])

    def across_cores(value):
        return lax.ppermute(value, "rep", [(0, 1), (1, 0)])

    def after(value, *others):
        return lax.optimization_barrier((value, *others))[0]

    smem = pl.BlockSpec(memory_space=pltpu.SMEM)
    vmem = pl.BlockSpec(memory_space=pltpu.VMEM)
    weights, places = pl.pallas_call(
        prep_kernel,
        out_shape=(
            jax.ShapeDtypeStruct((PLACES, TILE), jnp.float32),
            jax.ShapeDtypeStruct((PLACES,), jnp.int32),
        ),
        in_specs=[smem, vmem],
        out_specs=(vmem, smem),
    )(counts, gp_weights.reshape(-1, TILE))

    far0 = across_x(embeddings)
    near3 = across_z(embeddings, 3)
    near1 = across_z(embeddings, 1)
    half = enc_rows // 2
    head_mine = across_x(lax.dynamic_slice_in_dim(head_weight, rep * half, half, 0))
    head_other = across_cores(head_mine)
    far_head = jnp.where(
        rep == 0,
        jnp.concatenate([head_mine, head_other]),
        jnp.concatenate([head_other, head_mine]),
    )
    far0_next, weights, places = lax.optimization_barrier((far0, weights, places))
    near3, far_head = lax.optimization_barrier((near3, far_head))
    far2 = across_z(far0_next, 2)
    near2 = across_z(near3, 1)
    far1 = across_x(near1)
    far3 = across_x(near3)

    def features(near, far):
        value = jnp.dot(near, head_weight, preferred_element_type=jnp.float32)
        value += jnp.dot(far, far_head, preferred_element_type=jnp.float32)
        return value.astype(jnp.bfloat16)

    own0, own1 = features(embeddings, far0), features(near1, far1)
    other0, other1 = across_cores(own0), across_cores(own1)
    lent1 = across_cores(after(near1, own1))
    buffers = (
        jax.ShapeDtypeStruct((18 * TILE, width), jnp.bfloat16),
        jax.ShapeDtypeStruct((PLACES, TILE), jnp.float32),
        jax.ShapeDtypeStruct((12 * TILE, share_cols), jnp.bfloat16),
    )
    own2, own3 = features(near2, far2), features(near3, far3)
    other2, other3 = across_cores(own2), across_cores(own3)
    lent3 = across_cores(after(near3, own3))
    packed = pl.pallas_call(
        pack_kernel,
        out_shape=buffers,
        in_specs=[smem] + [vmem] * 11,
        out_specs=(vmem,) * 3,
        compiler_params=pltpu.CompilerParams(vmem_limit_bytes=30 * 2**20),
    )(
        places,
        embeddings,
        near1,
        near2,
        near3,
        lent1,
        own0,
        own1,
        own2,
        own3,
        other0,
        other1,
    )

    *_, own_grad, head_part, head_sent = pl.pallas_call(
        pair_kernel,
        out_shape=buffers
        + (
            jax.ShapeDtypeStruct((share_rows, width), jnp.bfloat16),
            jax.ShapeDtypeStruct((enc_rows, width), jnp.float32),
            jax.ShapeDtypeStruct((enc_rows, width), jnp.bfloat16),
        ),
        in_specs=[smem] + [vmem] * 7,
        out_specs=(vmem,) * 6,
        input_output_aliases={5: 0, 6: 1, 7: 2},
        scratch_shapes=[pltpu.VMEM((4 * CHUNK, width), jnp.bfloat16)],
        compiler_params=pltpu.CompilerParams(vmem_limit_bytes=40 * 2**20),
    )(places, weights, lent3, other2, other3, *packed)
    head_other_part = across_cores(head_sent)
    embed_grad = lax.dot_general(
        own_grad, head_weight, (((1,), (1,)), ((), ())), preferred_element_type=jnp.float32
    ).astype(jnp.bfloat16)
    head_grad = head_part + head_other_part.astype(jnp.float32)
    return embed_grad, head_grad


def solution(mesh):
    placed = (P(("groups", "loop", "rep"), "enc"), P("enc", None), P("groups"), P("groups"))
    sizes = dict(mesh.shape)

    def body(*arrays):
        share_rows = arrays[0].shape[0]
        small = sizes["loop"] == 4 and sizes["enc"] == 2 and sizes["rep"] == 2
        if small and share_rows == 2 * TILE:
            return gathered_body(*arrays)
        return ring_body(*arrays)

    return jax.shard_map(
        body,
        mesh=mesh,
        in_specs=placed,
        out_specs=(P(("groups", "loop", "rep"), "enc"), P(("groups", "enc"), None)),
        check_vma=False,
    )
```

profile of v0, /device:TPU:0, one launch (start us, length us, event | category | flops | bytes accessed | tf_op | source)
XLA Modules:
  0.0 42.2 jit_solution(11039097912621254680)
XLA Ops:
  0.6 0.0 copy-start
  0.6 1.1 %copy-done = bf16[384,768]{1,0:T(8,128)(2,1)S(1)} copy-done((bf16[384,768]{1,0:T(8,128)(2,1)S(1)}, bf16[384,768]{1,0:T(8,128)(2,1)}, u32[]{:S(2)}) %copy-start) | copy-done | bytes 589848
  1.7 3.0 %collective-permute-start.2 = (bf16[192,768]{1,0:T(8,128)(2,1)S(1)}, bf16[192,768]{1,0:T(8,128)(2,1)S(1)}, u32[]{:S(2)}, u32[]{:S(2)}) collective-permute-start(bf16[192,768]{1,0:T(8,128)(2,1)S(1)} %constant_dynamic-slice_fusion), channel_id=1, source_target_pairs={{0,2},{2,0},{1,3},{3,1},{4,6},{6,4},{5,7},{7,5},{8,10},{10,8},{9,1... | collective-permute-start | bytes 884744 | tf_op jit(solution)/shard_map/ppermute | solution.py:292
  4.7 1.6 %collective-permute-start.10 = (bf16[256,384]{1,0:T(8,128)(2,1)}, bf16[256,384]{1,0:T(8,128)(2,1)S(1)}, u32[]{:S(2)}, u32[]{:S(2)}) collective-permute-start(bf16[256,384]{1,0:T(8,128)(2,1)} %near0.1), channel_id=1, source_target_pairs={{0,4},{4,0},{8,12},{12,8},{1,5},{5,1},{9,13},{13,9},{2,6},{6,2},{1... | collective-permute-start | bytes 589832 | tf_op jit(solution)/shard_map/ppermute | solution.py:289
  6.3 2.5 %collective-permute-start.1 = (bf16[256,384]{1,0:T(8,128)(2,1)}, bf16[256,384]{1,0:T(8,128)(2,1)S(1)}, u32[]{:S(2)}, u32[]{:S(2)}) collective-permute-start(bf16[256,384]{1,0:T(8,128)(2,1)} %near0.1), channel_id=1, source_target_pairs={{0,12},{4,8},{8,4},{12,0},{1,13},{5,9},{9,5},{13,1},{2,14},{6,10},... | collective-permute-start | bytes 589832 | tf_op jit(solution)/shard_map/ppermute | solution.py:289
  8.8 0.5 %collective-permute-start = (bf16[256,384]{1,0:T(8,128)(2,1)}, bf16[256,384]{1,0:T(8,128)(2,1)S(1)}, u32[]{:S(2)}, u32[]{:S(2)}) collective-permute-start(bf16[256,384]{1,0:T(8,128)(2,1)} %near0.1), channel_id=1, source_target_pairs={{0,2},{2,0},{1,3},{3,1},{4,6},{6,4},{5,7},{7,5},{8,10},{10,8},{9,1... | collective-permute-start | bytes 589832 | tf_op jit(solution)/shard_map/ppermute | solution.py:292
  9.3 3.2 %collective-permute-done.2 = bf16[192,768]{1,0:T(8,128)(2,1)S(1)} collective-permute-done((bf16[192,768]{1,0:T(8,128)(2,1)S(1)}, bf16[192,768]{1,0:T(8,128)(2,1)S(1)}, u32[]{:S(2)}, u32[]{:S(2)}) %collective-permute-start.2) | collective-permute-done | bytes 294944 | tf_op jit(solution)/shard_map/ppermute | solution.py:292
  12.6 0.0 collective-permute-start.3
  12.6 1.3 %fusion.9 = f32[256,768]{1,0:T(8,128)S(1)} fusion(bf16[256,384]{1,0:T(8,128)(2,1)} %near0.1, bf16[384,768]{1,0:T(8,128)(2,1)S(1)} %copy-done), kind=kOutput, calls=%fused_computation.17 | convolution fusion | flops 150994944 | bytes 1572864 | tf_op jit(solution)/shard_map/dot_general | solution.py:331
  13.9 1.5 %shard_map.59 = (f32[24,128]{1,0:T(8,128)}, s32[24]{0:T(128)}) custom-call(s32[4]{0:T(128)} %counts_ref.1, f32[16,128]{1,0:T(8,128)} %bitcast.31), custom_call_target="tpu_custom_call" | custom-call | tf_op jit(solution)/shard_map/pallas_call | solution.py:302
  15.4 0.6 %collective-permute-done = bf16[256,384]{1,0:T(8,128)(2,1)S(1)} collective-permute-done((bf16[256,384]{1,0:T(8,128)(2,1)}, bf16[256,384]{1,0:T(8,128)(2,1)S(1)}, u32[]{:S(2)}, u32[]{:S(2)}) %collective-permute-start) | collective-permute-done | bytes 196640 | tf_op jit(solution)/shard_map/ppermute | solution.py:292
  15.9 2.8 %collective-permute-start.7 = (bf16[256,384]{1,0:T(8,128)(2,1)S(1)}, bf16[256,384]{1,0:T(8,128)(2,1)S(1)}, u32[]{:S(2)}, u32[]{:S(2)}) collective-permute-start(bf16[256,384]{1,0:T(8,128)(2,1)S(1)} %collective-permute-done), channel_id=1, source_target_pairs={{0,8},{4,12},{8,0},{12,4},{1,9},{5,13},{9,1},{13,5},{2,10},{6,14},... | collective-permute-start | bytes 589832 | tf_op jit(solution)/shard_map/ppermute | solution.py:289
  18.8 0.0 collective-permute-done.10.near1
  18.8 1.5 %collective-permute-start.11 = (bf16[256,384]{1,0:T(8,128)(2,1)S(1)}, bf16[256,384]{1,0:T(8,128)(2,1)S(1)}, u32[]{:S(2)}, u32[]{:S(2)}) collective-permute-start(bf16[256,384]{1,0:T(8,128)(2,1)S(1)} %collective-permute-done.10.near1), channel_id=1, source_target_pairs={{0,2},{2,0},{1,3},{3,1},{4,6},{6,4},{5,7},{7,5},{8,10},{10,8},{9,1... | collective-permute-start | bytes 589832 | tf_op jit(solution)/shard_map/ppermute | solution.py:292
  20.3 0.4 fusion.8
  20.6 0.0 collective-permute-done.3
  20.7 0.2 maximum_select_fusion
  20.8 0.0 collective-permute-done.1.near3
  20.9 1.6 %collective-permute-start.6 = (bf16[256,384]{1,0:T(8,128)(2,1)S(1)}, bf16[256,384]{1,0:T(8,128)(2,1)S(1)}, u32[]{:S(2)}, u32[]{:S(2)}) collective-permute-start(bf16[256,384]{1,0:T(8,128)(2,1)S(1)} %collective-permute-done.1.near3), channel_id=1, source_target_pairs={{0,4},{4,0},{8,12},{12,8},{1,5},{5,1},{9,13},{13,9},{2,6},{6,2},{1... | collective-permute-start | bytes 589832 | tf_op jit(solution)/shard_map/ppermute | solution.py:289
  22.5 0.5 %collective-permute-start.4 = (bf16[256,384]{1,0:T(8,128)(2,1)S(1)}, bf16[256,384]{1,0:T(8,128)(2,1)S(1)}, u32[]{:S(2)}, u32[]{:S(2)}) collective-permute-start(bf16[256,384]{1,0:T(8,128)(2,1)S(1)} %collective-permute-done.1.near3), channel_id=1, source_target_pairs={{0,2},{2,0},{1,3},{3,1},{4,6},{6,4},{5,7},{7,5},{8,10},{10,8},{9,1... | collective-permute-start | bytes 589832 | tf_op jit(solution)/shard_map/ppermute | solution.py:292
  23.0 3.5 %collective-permute-done.11 = bf16[256,384]{1,0:T(8,128)(2,1)S(1)} collective-permute-done((bf16[256,384]{1,0:T(8,128)(2,1)S(1)}, bf16[256,384]{1,0:T(8,128)(2,1)S(1)}, u32[]{:S(2)}, u32[]{:S(2)}) %collective-permute-start.11) | collective-permute-done | bytes 196640 | tf_op jit(solution)/shard_map/ppermute | solution.py:292
  26.6 0.4 fusion.2.own1
  26.9 0.1 collective-permute-start.14
  27.0 0.5 %collective-permute-start.12 = (bf16[256,384]{1,0:T(8,128)(2,1)S(1)}, bf16[256,384]{1,0:T(8,128)(2,1)S(1)}, u32[]{:S(2)}, u32[]{:S(2)}) collective-permute-start(bf16[256,384]{1,0:T(8,128)(2,1)S(1)} %collective-permute-done.10.near1), channel_id=1, source_target_pairs={{0,1},{1,0},{2,3},{3,2},{4,5},{5,4},{6,7},{7,6},{8,9},{9,8},{10,11... | collective-permute-start | bytes 589832 | tf_op jit(solution)/shard_map/ppermute | solution.py:295
  27.5 0.4 fusion.3.own0
  27.9 0.6 %collective-permute-done.7 = bf16[256,384]{1,0:T(8,128)(2,1)S(1)} collective-permute-done((bf16[256,384]{1,0:T(8,128)(2,1)S(1)}, bf16[256,384]{1,0:T(8,128)(2,1)S(1)}, u32[]{:S(2)}, u32[]{:S(2)}) %collective-permute-start.7) | collective-permute-done | bytes 196640 | tf_op jit(solution)/shard_map/ppermute | solution.py:289
  28.5 0.0 collective-permute-start.13
  28.5 0.4 fusion.7
  28.8 1.0 %collective-permute-done.4 = bf16[256,384]{1,0:T(8,128)(2,1)S(1)} collective-permute-done((bf16[256,384]{1,0:T(8,128)(2,1)S(1)}, bf16[256,384]{1,0:T(8,128)(2,1)S(1)}, u32[]{:S(2)}, u32[]{:S(2)}) %collective-permute-start.4) | collective-permute-done | bytes 196640 | tf_op jit(solution)/shard_map/ppermute | solution.py:292
  29.8 0.4 fusion.6
  30.2 0.4 fusion.4.own3
  30.6 0.0 copy-start.1
  30.6 0.0 copy-start.3
  30.6 0.1 collective-permute-start.9
  30.7 0.0 collective-permute-done.6.near2
  30.7 0.4 fusion.5.own2
  31.1 0.0 copy-start.2
  31.1 0.6 %collective-permute-start.8 = (bf16[256,768]{1,0:T(8,128)(2,1)S(1)}, bf16[256,768]{1,0:T(8,128)(2,1)S(1)}, u32[]{:S(2)}, u32[]{:S(2)}) collective-permute-start(bf16[256,768]{1,0:T(8,128)(2,1)S(1)} %fusion.5.own2), channel_id=1, source_target_pairs={{0,1},{1,0},{2,3},{3,2},{4,5},{5,4},{6,7},{7,6},{8,9},{9,8},{10,11... | collective-permute-start | bytes 1179656 | tf_op jit(solution)/shard_map/ppermute | solution.py:295
  31.6 0.0 collective-permute-done.12.lent1
  31.6 0.1 collective-permute-start.5
  31.7 1.5 %shard_map.60 = (bf16[2304,768]{1,0:T(8,128)(2,1)S(1)}, f32[24,128]{1,0:T(8,128)S(1)}, bf16[1536,384]{1,0:T(8,128)(2,1)S(1)}) custom-call(s32[24]{0:T(128)S(1)} %copy-done.3, bf16[256,384]{1,0:T(8,128)(2,1)S(1)} %copy-done.1, bf16[256,384]{1,0:T(8,128)(2,1)S(1)} %collective-permute-done.10.near1, bf16[256,384]{1,0:T(8,128)(2,1)S(1)} %collective-permute-done.6.near2, ...), custom_call_target="tpu_custom_call" | custom-call | tf_op jit(solution)/shard_map/pallas_call | solution.py:346
  33.3 0.0 collective-permute-done.5.lent3
  33.3 0.0 collective-permute-done.8.other2
  33.3 5.7 %shard_map.61 = (bf16[2304,768]{1,0:T(8,128)(2,1)S(1)}, f32[24,128]{1,0:T(8,128)S(1)}, bf16[1536,384]{1,0:T(8,128)(2,1)S(1)}, bf16[256,768]{1,0:T(8,128)(2,1)S(1...) custom-call(s32[24]{0:T(128)S(1)} %copy-done.3, ...), custom_call_target="tpu_custom_call", output_to_operand_aliasing={{0}: (5, {}), {1}: (6, {}), {2}: (7, {})} | custom-call | tf_op jit(solution)/shard_map/pallas_call | solution.py:367
  39.0 0.5 %collective-permute-start.15 = (bf16[384,768]{1,0:T(8,128)(2,1)S(1)}, bf16[384,768]{1,0:T(8,128)(2,1)S(1)}, u32[]{:S(2)}, u32[]{:S(2)}) collective-permute-start(bf16[384,768]{1,0:T(8,128)(2,1)S(1)} %get-tuple-element.31), channel_id=1, source_target_pairs={{0,1},{1,0},{2,3},{3,2},{4,5},{5,4},{6,7},{7,6},{8,9},{9,8},{10,11... | collective-permute-start | bytes 1769480 | tf_op jit(solution)/shard_map/ppermute | solution.py:295
  39.5 1.1 %convolution_convert_fusion = bf16[256,384]{1,0:T(8,128)(2,1)} fusion(bf16[256,768]{1,0:T(8,128)(2,1)S(1)} %get-tuple-element.29, bf16[384,768]{1,0:T(8,128)(2,1)S(1)} %copy-done), kind=kOutput, calls=%fused_computation.11 | convolution fusion | flops 151093248 | bytes 1179648 | tf_op jit(solution)/shard_map/dot_general | solution.py:382
  40.6 0.6 %collective-permute-done.15 = bf16[384,768]{1,0:T(8,128)(2,1)S(1)} collective-permute-done((bf16[384,768]{1,0:T(8,128)(2,1)S(1)}, bf16[384,768]{1,0:T(8,128)(2,1)S(1)}, u32[]{:S(2)}, u32[]{:S(2)}) %collective-permute-start.15) | collective-permute-done | bytes 589856 | tf_op jit(solution)/shard_map/ppermute | solution.py:295
  41.1 1.1 %convert_add_fusion = f32[384,768]{1,0:T(8,128)} fusion(f32[384,768]{1,0:T(8,128)S(1)} %get-tuple-element.30, bf16[384,768]{1,0:T(8,128)(2,1)S(1)} %collective-permute-done.15), kind=kLoop, calls=%fused_computation.10 | loop fusion | flops 589824 | bytes 2949120 | tf_op jit(solution)/shard_map/add | solution.py:385
  (7 shorter events, 0.0 us)
Async XLA Ops:
  0.6 1.1 %copy-start = (bf16[384,768]{1,0:T(8,128)(2,1)S(1)}, bf16[384,768]{1,0:T(8,128)(2,1)}, u32[]{:S(2)}) copy-start(bf16[384,768]{1,0:T(8,128)(2,1)} %param.5) | copy-start | bytes 1769476
  1.7 10.8 %collective-permute-start.2 = (bf16[192,768]{1,0:T(8,128)(2,1)S(1)}, bf16[192,768]{1,0:T(8,128)(2,1)S(1)}, u32[]{:S(2)}, u32[]{:S(2)}) collective-permute-start(bf16[192,768]{1,0:T(8,128)(2,1)S(1)} %constant_dynamic-slice_fusion), channel_id=1, source_target_pairs={{0,2},{2,0},{1,3},{3,1},{4,6},{6,4},{5,7},{7,5},{8,10},{10,8},{9,1... | collective-permute-start | bytes 884744 | tf_op jit(solution)/shard_map/ppermute | solution.py:292
  4.7 14.1 %collective-permute-start.10 = (bf16[256,384]{1,0:T(8,128)(2,1)}, bf16[256,384]{1,0:T(8,128)(2,1)S(1)}, u32[]{:S(2)}, u32[]{:S(2)}) collective-permute-start(bf16[256,384]{1,0:T(8,128)(2,1)} %near0.1), channel_id=1, source_target_pairs={{0,4},{4,0},{8,12},{12,8},{1,5},{5,1},{9,13},{13,9},{2,6},{6,2},{1... | collective-permute-start | bytes 589832 | tf_op jit(solution)/shard_map/ppermute | solution.py:289
  6.3 14.5 %collective-permute-start.1 = (bf16[256,384]{1,0:T(8,128)(2,1)}, bf16[256,384]{1,0:T(8,128)(2,1)S(1)}, u32[]{:S(2)}, u32[]{:S(2)}) collective-permute-start(bf16[256,384]{1,0:T(8,128)(2,1)} %near0.1), channel_id=1, source_target_pairs={{0,12},{4,8},{8,4},{12,0},{1,13},{5,9},{9,5},{13,1},{2,14},{6,10},... | collective-permute-start | bytes 589832 | tf_op jit(solution)/shard_map/ppermute | solution.py:289
  8.8 7.2 %collective-permute-start = (bf16[256,384]{1,0:T(8,128)(2,1)}, bf16[256,384]{1,0:T(8,128)(2,1)S(1)}, u32[]{:S(2)}, u32[]{:S(2)}) collective-permute-start(bf16[256,384]{1,0:T(8,128)(2,1)} %near0.1), channel_id=1, source_target_pairs={{0,2},{2,0},{1,3},{3,1},{4,6},{6,4},{5,7},{7,5},{8,10},{10,8},{9,1... | collective-permute-start | bytes 589832 | tf_op jit(solution)/shard_map/ppermute | solution.py:292
  12.6 8.1 %collective-permute-start.3 = (bf16[192,768]{1,0:T(8,128)(2,1)S(1)}, bf16[192,768]{1,0:T(8,128)(2,1)S(1)}, u32[]{:S(2)}, u32[]{:S(2)}) collective-permute-start(bf16[192,768]{1,0:T(8,128)(2,1)S(1)} %collective-permute-done.2), channel_id=1, source_target_pairs={{0,1},{1,0},{2,3},{3,2},{4,5},{5,4},{6,7},{7,6},{8,9},{9,8},{10,11... | collective-permute-start | bytes 884744 | tf_op jit(solution)/shard_map/ppermute | solution.py:295
  15.9 12.5 %collective-permute-start.7 = (bf16[256,384]{1,0:T(8,128)(2,1)S(1)}, bf16[256,384]{1,0:T(8,128)(2,1)S(1)}, u32[]{:S(2)}, u32[]{:S(2)}) collective-permute-start(bf16[256,384]{1,0:T(8,128)(2,1)S(1)} %collective-permute-done), channel_id=1, source_target_pairs={{0,8},{4,12},{8,0},{12,4},{1,9},{5,13},{9,1},{13,5},{2,10},{6,14},... | collective-permute-start | bytes 589832 | tf_op jit(solution)/shard_map/ppermute | solution.py:289
  18.8 7.8 %collective-permute-start.11 = (bf16[256,384]{1,0:T(8,128)(2,1)S(1)}, bf16[256,384]{1,0:T(8,128)(2,1)S(1)}, u32[]{:S(2)}, u32[]{:S(2)}) collective-permute-start(bf16[256,384]{1,0:T(8,128)(2,1)S(1)} %collective-permute-done.10.near1), channel_id=1, source_target_pairs={{0,2},{2,0},{1,3},{3,1},{4,6},{6,4},{5,7},{7,5},{8,10},{10,8},{9,1... | collective-permute-start | bytes 589832 | tf_op jit(solution)/shard_map/ppermute | solution.py:292
  20.9 9.8 %collective-permute-start.6 = (bf16[256,384]{1,0:T(8,128)(2,1)S(1)}, bf16[256,384]{1,0:T(8,128)(2,1)S(1)}, u32[]{:S(2)}, u32[]{:S(2)}) collective-permute-start(bf16[256,384]{1,0:T(8,128)(2,1)S(1)} %collective-permute-done.1.near3), channel_id=1, source_target_pairs={{0,4},{4,0},{8,12},{12,8},{1,5},{5,1},{9,13},{13,9},{2,6},{6,2},{1... | collective-permute-start | bytes 589832 | tf_op jit(solution)/shard_map/ppermute | solution.py:289
  22.5 7.3 %collective-permute-start.4 = (bf16[256,384]{1,0:T(8,128)(2,1)S(1)}, bf16[256,384]{1,0:T(8,128)(2,1)S(1)}, u32[]{:S(2)}, u32[]{:S(2)}) collective-permute-start(bf16[256,384]{1,0:T(8,128)(2,1)S(1)} %collective-permute-done.1.near3), channel_id=1, source_target_pairs={{0,2},{2,0},{1,3},{3,1},{4,6},{6,4},{5,7},{7,5},{8,10},{10,8},{9,1... | collective-permute-start | bytes 589832 | tf_op jit(solution)/shard_map/ppermute | solution.py:292
  26.9 4.8 %collective-permute-start.14 = (bf16[256,768]{1,0:T(8,128)(2,1)S(1)}, bf16[256,768]{1,0:T(8,128)(2,1)S(1)}, u32[]{:S(2)}, u32[]{:S(2)}) collective-permute-start(bf16[256,768]{1,0:T(8,128)(2,1)S(1)} %fusion.2.own1), channel_id=1, source_target_pairs={{0,1},{1,0},{2,3},{3,2},{4,5},{5,4},{6,7},{7,6},{8,9},{9,8},{10,11... | collective-permute-start | bytes 1179656 | tf_op jit(solution)/shard_map/ppermute | solution.py:295
  27.0 4.6 %collective-permute-start.12 = (bf16[256,384]{1,0:T(8,128)(2,1)S(1)}, bf16[256,384]{1,0:T(8,128)(2,1)S(1)}, u32[]{:S(2)}, u32[]{:S(2)}) collective-permute-start(bf16[256,384]{1,0:T(8,128)(2,1)S(1)} %collective-permute-done.10.near1), channel_id=1, source_target_pairs={{0,1},{1,0},{2,3},{3,2},{4,5},{5,4},{6,7},{7,6},{8,9},{9,8},{10,11... | collective-permute-start | bytes 589832 | tf_op jit(solution)/shard_map/ppermute | solution.py:295
  28.5 3.2 %collective-permute-start.13 = (bf16[256,768]{1,0:T(8,128)(2,1)S(1)}, bf16[256,768]{1,0:T(8,128)(2,1)S(1)}, u32[]{:S(2)}, u32[]{:S(2)}) collective-permute-start(bf16[256,768]{1,0:T(8,128)(2,1)S(1)} %fusion.3.own0), channel_id=1, source_target_pairs={{0,1},{1,0},{2,3},{3,2},{4,5},{5,4},{6,7},{7,6},{8,9},{9,8},{10,11... | collective-permute-start | bytes 1179656 | tf_op jit(solution)/shard_map/ppermute | solution.py:295
  30.6 1.2 %copy-start.1 = (bf16[256,384]{1,0:T(8,128)(2,1)S(1)}, bf16[256,384]{1,0:T(8,128)(2,1)}, u32[]{:S(2)}) copy-start(bf16[256,384]{1,0:T(8,128)(2,1)} %near0.1) | copy-start | bytes 589828
  30.6 1.1 %copy-start.3 = (s32[24]{0:T(128)S(1)}, s32[24]{0:T(128)}, u32[]{:S(2)}) copy-start(s32[24]{0:T(128)} %get-tuple-element.19.places) | copy-start | bytes 292
  30.6 2.7 %collective-permute-start.9 = (bf16[256,768]{1,0:T(8,128)(2,1)S(1)}, bf16[256,768]{1,0:T(8,128)(2,1)S(1)}, u32[]{:S(2)}, u32[]{:S(2)}) collective-permute-start(bf16[256,768]{1,0:T(8,128)(2,1)S(1)} %fusion.4.own3), channel_id=1, source_target_pairs={{0,1},{1,0},{2,3},{3,2},{4,5},{5,4},{6,7},{7,6},{8,9},{9,8},{10,11... | collective-permute-start | bytes 1179656 | tf_op jit(solution)/shard_map/ppermute | solution.py:295
  31.1 2.2 %copy-start.2 = (f32[24,128]{1,0:T(8,128)S(1)}, f32[24,128]{1,0:T(8,128)}, u32[]{:S(2)}) copy-start(f32[24,128]{1,0:T(8,128)} %get-tuple-element.20.weights) | copy-start | bytes 36868
  31.1 2.2 %collective-permute-start.8 = (bf16[256,768]{1,0:T(8,128)(2,1)S(1)}, bf16[256,768]{1,0:T(8,128)(2,1)S(1)}, u32[]{:S(2)}, u32[]{:S(2)}) collective-permute-start(bf16[256,768]{1,0:T(8,128)(2,1)S(1)} %fusion.5.own2), channel_id=1, source_target_pairs={{0,1},{1,0},{2,3},{3,2},{4,5},{5,4},{6,7},{7,6},{8,9},{9,8},{10,11... | collective-permute-start | bytes 1179656 | tf_op jit(solution)/shard_map/ppermute | solution.py:295
  31.6 1.6 %collective-permute-start.5 = (bf16[256,384]{1,0:T(8,128)(2,1)S(1)}, bf16[256,384]{1,0:T(8,128)(2,1)S(1)}, u32[]{:S(2)}, u32[]{:S(2)}) collective-permute-start(bf16[256,384]{1,0:T(8,128)(2,1)S(1)} %collective-permute-done.1.near3), channel_id=1, source_target_pairs={{0,1},{1,0},{2,3},{3,2},{4,5},{5,4},{6,7},{7,6},{8,9},{9,8},{10,11... | collective-permute-start | bytes 589832 | tf_op jit(solution)/shard_map/ppermute | solution.py:295
  39.0 2.1 %collective-permute-start.15 = (bf16[384,768]{1,0:T(8,128)(2,1)S(1)}, bf16[384,768]{1,0:T(8,128)(2,1)S(1)}, u32[]{:S(2)}, u32[]{:S(2)}) collective-permute-start(bf16[384,768]{1,0:T(8,128)(2,1)S(1)} %get-tuple-element.31), channel_id=1, source_target_pairs={{0,1},{1,0},{2,3},{3,2},{4,5},{5,4},{6,7},{7,6},{8,9},{9,8},{10,11... | collective-permute-start | bytes 1769480 | tf_op jit(solution)/shard_map/ppermute | solution.py:295
where the time goes:
time: 42.4 us; the launch traced here: 42.2 us
  starting transfers between devices  15.9 us (38%)
  waiting for transfers between devices  9.53 us (22%)
  Pallas kernels  8.66 us (20%)
  matrix products  4.92 us (12%)
  other arithmetic  1.29 us (3%)
  local copies, waits for them, and re-layouts  1.1 us (3%)
  between operations  0.84 us (2%)
    ppermute x4, starting transfers between devices, across_z(): lax.ppermute(value, 'loop', [(i, i ^ step) for i in range(loop_size)])  8.53 us
    ppermute x4, waiting for transfers between devices, across_x(): return lax.ppermute(value, 'enc', [(0, 1), (1, 0)])  8.35 us
    pallas_call x1, Pallas kernels, gathered_body(): pl.pallas_call(pair_kernel, out_shape=buffers + (jax.ShapeDtypeStruct((sh...  5.66 us
    ppermute x4, starting transfers between devices, across_x(): return lax.ppermute(value, 'enc', [(0, 1), (1, 0)])  5.57 us
    dot_general x4, matrix products, features(): value = jnp.dot(near, head_weight, preferred_element_type=jnp.float32)  2.38 us
    ppermute x8, starting transfers between devices, across_cores(): return lax.ppermute(value, 'rep', [(0, 1), (1, 0)])  1.79 us
    pallas_call x1, Pallas kernels, gathered_body(): pl.pallas_call(pack_kernel, out_shape=buffers, in_specs=[smem] + [vmem] *...  1.52 us
    pallas_call x1, Pallas kernels, gathered_body(): pl.pallas_call(prep_kernel, out_shape=(jax.ShapeDtypeStruct((PLACES, TILE...  1.48 us
  transfers between devices with their start and end apart: 16, of which 6 were waited for; matrix products, arithmetic and copies ran while one was open for 12% of the time, Pallas kernels for 7%

commit v1 on v0

--- a/solution.py
+++ b/solution.py
@@ -207,7 +207,6 @@
     norms,
     near,
     own_out,
-    head_out,
     head_sent,
     grads,
 ):
@@ -271,7 +270,6 @@
                 (((0,), (0,)), ((), ())),
                 preferred_element_type=jnp.float32,
             )
-            head_out[...] = head
             head_sent[...] = head.astype(jnp.bfloat16)
 
     own = grads[:CHUNK, :]
@@ -364,16 +362,15 @@
         other1,
     )
 
-    *_, own_grad, head_part, head_sent = pl.pallas_call(
+    *_, own_grad, head_sent = pl.pallas_call(
         pair_kernel,
         out_shape=buffers
         + (
             jax.ShapeDtypeStruct((share_rows, width), jnp.bfloat16),
-            jax.ShapeDtypeStruct((enc_rows, width), jnp.float32),
             jax.ShapeDtypeStruct((enc_rows, width), jnp.bfloat16),
         ),
         in_specs=[smem] + [vmem] * 7,
-        out_specs=(vmem,) * 6,
+        out_specs=(vmem,) * 5,
         input_output_aliases={5: 0, 6: 1, 7: 2},
         scratch_shapes=[pltpu.VMEM((4 * CHUNK, width), jnp.bfloat16)],
         compiler_params=pltpu.CompilerParams(vmem_limit_bytes=40 * 2**20),
@@ -382,7 +379,7 @@
     embed_grad = lax.dot_general(
         own_grad, head_weight, (((1,), (1,)), ((), ())), preferred_element_type=jnp.float32
     ).astype(jnp.bfloat16)
-    head_grad = head_part + head_other_part.astype(jnp.float32)
+    head_grad = head_sent.astype(jnp.float32) + head_other_part.astype(jnp.float32)
     return embed_grad, head_grad
 
 

time: 42.4 us -> 42.5 us (level)
  waiting for transfers between devices: 9.53 us -> 9.98 us
    ppermute x8, waiting for transfers between devices: 0.57 us -> 1.03 us  [across_cores(): return lax.ppermute(value, 'rep', [(0, 1), (1, 0)])]
    ppermute x8, starting transfers between devices: 1.79 us -> 1.36 us  [across_cores(): return lax.ppermute(value, 'rep', [(0, 1), (1, 0)])]
  transfers between devices with their start and end apart: 16 -> 16, of which waited for: 6 -> 7; matrix products, arithmetic and copies ran while one was open for 12% -> 12% of each run, Pallas kernels for 7% -> 7%
where the time goes in v1:
time: 42.5 us; the launch traced here: 42.1 us
  starting transfers between devices  15.5 us (36%)
  waiting for transfers between devices  9.98 us (23%)
  Pallas kernels  8.56 us (20%)
  matrix products  4.92 us (12%)
  other arithmetic  1.31 us (3%)
  local copies, waits for them, and re-layouts  1.1 us (3%)
  between operations  0.82 us (2%)
    ppermute x4, starting transfers between devices, across_z(): lax.ppermute(value, 'loop', [(i, i ^ step) for i in range(loop_size)])  8.53 us
    ppermute x4, waiting for transfers between devices, across_x(): return lax.ppermute(value, 'enc', [(0, 1), (1, 0)])  8.35 us
    pallas_call x1, Pallas kernels, gathered_body(): pl.pallas_call(pair_kernel, out_shape=buffers + (jax.ShapeDtypeStruct((sh...  5.66 us
    ppermute x4, starting transfers between devices, across_x(): return lax.ppermute(value, 'enc', [(0, 1), (1, 0)])  5.57 us
    dot_general x4, matrix products, features(): value = jnp.dot(near, head_weight, preferred_element_type=jnp.float32)  2.38 us
    pallas_call x1, Pallas kernels, gathered_body(): pl.pallas_call(prep_kernel, out_shape=(jax.ShapeDtypeStruct((PLACES, TILE...  1.48 us
    dot_general x4, matrix products, features(): value += jnp.dot(far, far_head, preferred_element_type=jnp.float32)  1.46 us
    pallas_call x1, Pallas kernels, gathered_body(): pl.pallas_call(pack_kernel, out_shape=buffers, in_specs=[smem] + [vmem] *...  1.42 us
  transfers between devices with their start and end apart: 16, of which 7 were waited for; matrix products, arithmetic and copies ran while one was open for 12% of the time, Pallas kernels for 7%

profile of v1, /device:TPU:0, one launch (start us, length us, event | category | flops | bytes accessed | tf_op | source)
XLA Modules:
  0.0 42.1 jit_solution(874908515075797348)
XLA Ops:
  0.6 0.0 copy-start
  0.6 1.1 %copy-done = bf16[384,768]{1,0:T(8,128)(2,1)S(1)} copy-done((bf16[384,768]{1,0:T(8,128)(2,1)S(1)}, bf16[384,768]{1,0:T(8,128)(2,1)}, u32[]{:S(2)}) %copy-start) | copy-done | bytes 589848
  1.7 3.0 %collective-permute-start.2 = (bf16[192,768]{1,0:T(8,128)(2,1)S(1)}, bf16[192,768]{1,0:T(8,128)(2,1)S(1)}, u32[]{:S(2)}, u32[]{:S(2)}) collective-permute-start(bf16[192,768]{1,0:T(8,128)(2,1)S(1)} %constant_dynamic-slice_fusion), channel_id=1, source_target_pairs={{0,2},{2,0},{1,3},{3,1},{4,6},{6,4},{5,7},{7,5},{8,10},{10,8},{9,1... | collective-permute-start | bytes 884744 | tf_op jit(solution)/shard_map/ppermute | solution.py:290
  4.7 1.6 %collective-permute-start.10 = (bf16[256,384]{1,0:T(8,128)(2,1)}, bf16[256,384]{1,0:T(8,128)(2,1)S(1)}, u32[]{:S(2)}, u32[]{:S(2)}) collective-permute-start(bf16[256,384]{1,0:T(8,128)(2,1)} %near0.1), channel_id=1, source_target_pairs={{0,4},{4,0},{8,12},{12,8},{1,5},{5,1},{9,13},{13,9},{2,6},{6,2},{1... | collective-permute-start | bytes 589832 | tf_op jit(solution)/shard_map/ppermute | solution.py:287
  6.3 2.5 %collective-permute-start.1 = (bf16[256,384]{1,0:T(8,128)(2,1)}, bf16[256,384]{1,0:T(8,128)(2,1)S(1)}, u32[]{:S(2)}, u32[]{:S(2)}) collective-permute-start(bf16[256,384]{1,0:T(8,128)(2,1)} %near0.1), channel_id=1, source_target_pairs={{0,12},{4,8},{8,4},{12,0},{1,13},{5,9},{9,5},{13,1},{2,14},{6,10},... | collective-permute-start | bytes 589832 | tf_op jit(solution)/shard_map/ppermute | solution.py:287
  8.8 0.5 %collective-permute-start = (bf16[256,384]{1,0:T(8,128)(2,1)}, bf16[256,384]{1,0:T(8,128)(2,1)S(1)}, u32[]{:S(2)}, u32[]{:S(2)}) collective-permute-start(bf16[256,384]{1,0:T(8,128)(2,1)} %near0.1), channel_id=1, source_target_pairs={{0,2},{2,0},{1,3},{3,1},{4,6},{6,4},{5,7},{7,5},{8,10},{10,8},{9,1... | collective-permute-start | bytes 589832 | tf_op jit(solution)/shard_map/ppermute | solution.py:290
  9.3 3.2 %collective-permute-done.2 = bf16[192,768]{1,0:T(8,128)(2,1)S(1)} collective-permute-done((bf16[192,768]{1,0:T(8,128)(2,1)S(1)}, bf16[192,768]{1,0:T(8,128)(2,1)S(1)}, u32[]{:S(2)}, u32[]{:S(2)}) %collective-permute-start.2) | collective-permute-done | bytes 294944 | tf_op jit(solution)/shard_map/ppermute | solution.py:290
  12.6 0.0 collective-permute-start.3
  12.6 1.3 %fusion.9 = f32[256,768]{1,0:T(8,128)S(1)} fusion(bf16[256,384]{1,0:T(8,128)(2,1)} %near0.1, bf16[384,768]{1,0:T(8,128)(2,1)S(1)} %copy-done), kind=kOutput, calls=%fused_computation.17 | convolution fusion | flops 150994944 | bytes 1572864 | tf_op jit(solution)/shard_map/dot_general | solution.py:329
  13.9 1.5 %shard_map.59 = (f32[24,128]{1,0:T(8,128)}, s32[24]{0:T(128)}) custom-call(s32[4]{0:T(128)} %counts_ref.1, f32[16,128]{1,0:T(8,128)} %bitcast.31), custom_call_target="tpu_custom_call" | custom-call | tf_op jit(solution)/shard_map/pallas_call | solution.py:300
  15.4 0.6 %collective-permute-done = bf16[256,384]{1,0:T(8,128)(2,1)S(1)} collective-permute-done((bf16[256,384]{1,0:T(8,128)(2,1)}, bf16[256,384]{1,0:T(8,128)(2,1)S(1)}, u32[]{:S(2)}, u32[]{:S(2)}) %collective-permute-start) | collective-permute-done | bytes 196640 | tf_op jit(solution)/shard_map/ppermute | solution.py:290
  15.9 2.8 %collective-permute-start.7 = (bf16[256,384]{1,0:T(8,128)(2,1)S(1)}, bf16[256,384]{1,0:T(8,128)(2,1)S(1)}, u32[]{:S(2)}, u32[]{:S(2)}) collective-permute-start(bf16[256,384]{1,0:T(8,128)(2,1)S(1)} %collective-permute-done), channel_id=1, source_target_pairs={{0,8},{4,12},{8,0},{12,4},{1,9},{5,13},{9,1},{13,5},{2,10},{6,14},... | collective-permute-start | bytes 589832 | tf_op jit(solution)/shard_map/ppermute | solution.py:287
  18.8 0.0 collective-permute-done.10.near1
  18.8 1.5 %collective-permute-start.11 = (bf16[256,384]{1,0:T(8,128)(2,1)S(1)}, bf16[256,384]{1,0:T(8,128)(2,1)S(1)}, u32[]{:S(2)}, u32[]{:S(2)}) collective-permute-start(bf16[256,384]{1,0:T(8,128)(2,1)S(1)} %collective-permute-done.10.near1), channel_id=1, source_target_pairs={{0,2},{2,0},{1,3},{3,1},{4,6},{6,4},{5,7},{7,5},{8,10},{10,8},{9,1... | collective-permute-start | bytes 589832 | tf_op jit(solution)/shard_map/ppermute | solution.py:290
  20.3 0.4 fusion.8
  20.7 0.2 maximum_select_fusion
  20.8 0.0 collective-permute-done.1.near3
  20.9 1.6 %collective-permute-start.6 = (bf16[256,384]{1,0:T(8,128)(2,1)S(1)}, bf16[256,384]{1,0:T(8,128)(2,1)S(1)}, u32[]{:S(2)}, u32[]{:S(2)}) collective-permute-start(bf16[256,384]{1,0:T(8,128)(2,1)S(1)} %collective-permute-done.1.near3), channel_id=1, source_target_pairs={{0,4},{4,0},{8,12},{12,8},{1,5},{5,1},{9,13},{13,9},{2,6},{6,2},{1... | collective-permute-start | bytes 589832 | tf_op jit(solution)/shard_map/ppermute | solution.py:287
  22.5 0.5 %collective-permute-start.4 = (bf16[256,384]{1,0:T(8,128)(2,1)S(1)}, bf16[256,384]{1,0:T(8,128)(2,1)S(1)}, u32[]{:S(2)}, u32[]{:S(2)}) collective-permute-start(bf16[256,384]{1,0:T(8,128)(2,1)S(1)} %collective-permute-done.1.near3), channel_id=1, source_target_pairs={{0,2},{2,0},{1,3},{3,1},{4,6},{6,4},{5,7},{7,5},{8,10},{10,8},{9,1... | collective-permute-start | bytes 589832 | tf_op jit(solution)/shard_map/ppermute | solution.py:290
  23.0 3.5 %collective-permute-done.11 = bf16[256,384]{1,0:T(8,128)(2,1)S(1)} collective-permute-done((bf16[256,384]{1,0:T(8,128)(2,1)S(1)}, bf16[256,384]{1,0:T(8,128)(2,1)S(1)}, u32[]{:S(2)}, u32[]{:S(2)}) %collective-permute-start.11) | collective-permute-done | bytes 196640 | tf_op jit(solution)/shard_map/ppermute | solution.py:290
  26.6 0.4 fusion.2.own1
  26.9 0.1 collective-permute-start.14
  27.0 0.5 %collective-permute-start.12 = (bf16[256,384]{1,0:T(8,128)(2,1)S(1)}, bf16[256,384]{1,0:T(8,128)(2,1)S(1)}, u32[]{:S(2)}, u32[]{:S(2)}) collective-permute-start(bf16[256,384]{1,0:T(8,128)(2,1)S(1)} %collective-permute-done.10.near1), channel_id=1, source_target_pairs={{0,1},{1,0},{2,3},{3,2},{4,5},{5,4},{6,7},{7,6},{8,9},{9,8},{10,11... | collective-permute-start | bytes 589832 | tf_op jit(solution)/shard_map/ppermute | solution.py:293
  27.5 0.4 fusion.3.own0
  27.9 0.6 %collective-permute-done.7 = bf16[256,384]{1,0:T(8,128)(2,1)S(1)} collective-permute-done((bf16[256,384]{1,0:T(8,128)(2,1)S(1)}, bf16[256,384]{1,0:T(8,128)(2,1)S(1)}, u32[]{:S(2)}, u32[]{:S(2)}) %collective-permute-start.7) | collective-permute-done | bytes 196640 | tf_op jit(solution)/shard_map/ppermute | solution.py:287
  28.5 0.0 collective-permute-start.13
  28.5 0.4 fusion.7
  28.8 1.0 %collective-permute-done.4 = bf16[256,384]{1,0:T(8,128)(2,1)S(1)} collective-permute-done((bf16[256,384]{1,0:T(8,128)(2,1)S(1)}, bf16[256,384]{1,0:T(8,128)(2,1)S(1)}, u32[]{:S(2)}, u32[]{:S(2)}) %collective-permute-start.4) | collective-permute-done | bytes 196640 | tf_op jit(solution)/shard_map/ppermute | solution.py:290
  29.8 0.4 fusion.6
  30.2 0.4 fusion.4.own3
  30.6 0.0 copy-start.1
  30.6 0.0 copy-start.3
  30.6 0.1 collective-permute-start.9
  30.7 0.0 collective-permute-done.6.near2
  30.7 0.4 fusion.5.own2
  31.1 0.0 copy-start.2
  31.1 0.6 %collective-permute-start.8 = (bf16[256,768]{1,0:T(8,128)(2,1)S(1)}, bf16[256,768]{1,0:T(8,128)(2,1)S(1)}, u32[]{:S(2)}, u32[]{:S(2)}) collective-permute-start(bf16[256,768]{1,0:T(8,128)(2,1)S(1)} %fusion.5.own2), channel_id=1, source_target_pairs={{0,1},{1,0},{2,3},{3,2},{4,5},{5,4},{6,7},{7,6},{8,9},{9,8},{10,11... | collective-permute-start | bytes 1179656 | tf_op jit(solution)/shard_map/ppermute | solution.py:293
  31.6 0.1 collective-permute-start.5
  31.7 0.0 collective-permute-done.14.other1
  31.7 0.0 collective-permute-done.13.other0
  31.7 1.4 %shard_map.60 = (bf16[2304,768]{1,0:T(8,128)(2,1)S(1)}, f32[24,128]{1,0:T(8,128)S(1)}, bf16[1536,384]{1,0:T(8,128)(2,1)S(1)}) custom-call(s32[24]{0:T(128)S(1)} %copy-done.3, bf16[256,384]{1,0:T(8,128)(2,1)S(1)} %copy-done.1, bf16[256,384]{1,0:T(8,128)(2,1)S(1)} %collective-permute-done.10.near1, bf16[256,384]{1,0:T(8,128)(2,1)S(1)} %collective-permute-done.6.near2, ...), custom_call_target="tpu_custom_call" | custom-call | tf_op jit(solution)/shard_map/pallas_call | solution.py:344
  33.2 0.1 collective-permute-done.5.lent3
  33.3 0.0 collective-permute-done.9.other3
  33.3 5.7 %shard_map.61 = (bf16[2304,768]{1,0:T(8,128)(2,1)S(1)}, f32[24,128]{1,0:T(8,128)S(1)}, bf16[1536,384]{1,0:T(8,128)(2,1)S(1)}, bf16[256,768]{1,0:T(8,128)(2,1)S(1)}, bf16[384,768]{1,0:T(8,128)(2,1)S(1)}) custom-call(s32[24]{0:T(128)S(1)} %copy-done.3, f32[24,128]{1,0:T(8,128)S(1)} %copy-done.2, ...), custom_call_target="tpu_custom_call", output_to_operand_aliasing={{0}: (5, {}), {1}: (6, {}), {2}: (7, {})} | custom-call | tf_op jit(solution)/shard_map/pallas_call | solution.py:365
  38.9 0.1 collective-permute-start.15
  39.0 1.1 %convolution_convert_fusion = bf16[256,384]{1,0:T(8,128)(2,1)} fusion(bf16[256,768]{1,0:T(8,128)(2,1)S(1)} %get-tuple-element.28, bf16[384,768]{1,0:T(8,128)(2,1)S(1)} %copy-done), kind=kOutput, calls=%fused_computation.11 | convolution fusion | flops 151093248 | bytes 1179648 | tf_op jit(solution)/shard_map/dot_general | solution.py:379
  40.1 0.9 %collective-permute-done.15 = bf16[384,768]{1,0:T(8,128)(2,1)S(1)} collective-permute-done((bf16[384,768]{1,0:T(8,128)(2,1)S(1)}, bf16[384,768]{1,0:T(8,128)(2,1)S(1)}, u32[]{:S(2)}, u32[]{:S(2)}) %collective-permute-start.15) | collective-permute-done | bytes 589856 | tf_op jit(solution)/shard_map/ppermute | solution.py:293
  41.0 1.1 %convert_add_fusion = f32[384,768]{1,0:T(8,128)} fusion(bf16[384,768]{1,0:T(8,128)(2,1)S(1)} %collective-permute-done.15, bf16[384,768]{1,0:T(8,128)(2,1)S(1)} %get-tuple-element.29), kind=kLoop, calls=%fused_computation.10 | loop fusion | flops 884736 | bytes 2359296 | tf_op jit(solution)/shard_map/add | solution.py:382
  (7 shorter events, 0.0 us)
Async XLA Ops:
  0.6 1.1 %copy-start = (bf16[384,768]{1,0:T(8,128)(2,1)S(1)}, bf16[384,768]{1,0:T(8,128)(2,1)}, u32[]{:S(2)}) copy-start(bf16[384,768]{1,0:T(8,128)(2,1)} %param.5) | copy-start | bytes 1769476
  1.7 10.8 %collective-permute-start.2 = (bf16[192,768]{1,0:T(8,128)(2,1)S(1)}, bf16[192,768]{1,0:T(8,128)(2,1)S(1)}, u32[]{:S(2)}, u32[]{:S(2)}) collective-permute-start(bf16[192,768]{1,0:T(8,128)(2,1)S(1)} %constant_dynamic-slice_fusion), channel_id=1, source_target_pairs={{0,2},{2,0},{1,3},{3,1},{4,6},{6,4},{5,7},{7,5},{8,10},{10,8},{9,1... | collective-permute-start | bytes 884744 | tf_op jit(solution)/shard_map/ppermute | solution.py:290
  4.7 14.1 %collective-permute-start.10 = (bf16[256,384]{1,0:T(8,128)(2,1)}, bf16[256,384]{1,0:T(8,128)(2,1)S(1)}, u32[]{:S(2)}, u32[]{:S(2)}) collective-permute-start(bf16[256,384]{1,0:T(8,128)(2,1)} %near0.1), channel_id=1, source_target_pairs={{0,4},{4,0},{8,12},{12,8},{1,5},{5,1},{9,13},{13,9},{2,6},{6,2},{1... | collective-permute-start | bytes 589832 | tf_op jit(solution)/shard_map/ppermute | solution.py:287
  6.3 14.5 %collective-permute-start.1 = (bf16[256,384]{1,0:T(8,128)(2,1)}, bf16[256,384]{1,0:T(8,128)(2,1)S(1)}, u32[]{:S(2)}, u32[]{:S(2)}) collective-permute-start(bf16[256,384]{1,0:T(8,128)(2,1)} %near0.1), channel_id=1, source_target_pairs={{0,12},{4,8},{8,4},{12,0},{1,13},{5,9},{9,5},{13,1},{2,14},{6,10},... | collective-permute-start | bytes 589832 | tf_op jit(solution)/shard_map/ppermute | solution.py:287
  8.8 7.2 %collective-permute-start = (bf16[256,384]{1,0:T(8,128)(2,1)}, bf16[256,384]{1,0:T(8,128)(2,1)S(1)}, u32[]{:S(2)}, u32[]{:S(2)}) collective-permute-start(bf16[256,384]{1,0:T(8,128)(2,1)} %near0.1), channel_id=1, source_target_pairs={{0,2},{2,0},{1,3},{3,1},{4,6},{6,4},{5,7},{7,5},{8,10},{10,8},{9,1... | collective-permute-start | bytes 589832 | tf_op jit(solution)/shard_map/ppermute | solution.py:290
  12.6 8.1 %collective-permute-start.3 = (bf16[192,768]{1,0:T(8,128)(2,1)S(1)}, bf16[192,768]{1,0:T(8,128)(2,1)S(1)}, u32[]{:S(2)}, u32[]{:S(2)}) collective-permute-start(bf16[192,768]{1,0:T(8,128)(2,1)S(1)} %collective-permute-done.2), channel_id=1, source_target_pairs={{0,1},{1,0},{2,3},{3,2},{4,5},{5,4},{6,7},{7,6},{8,9},{9,8},{10,11... | collective-permute-start | bytes 884744 | tf_op jit(solution)/shard_map/ppermute | solution.py:293
  15.9 12.5 %collective-permute-start.7 = (bf16[256,384]{1,0:T(8,128)(2,1)S(1)}, bf16[256,384]{1,0:T(8,128)(2,1)S(1)}, u32[]{:S(2)}, u32[]{:S(2)}) collective-permute-start(bf16[256,384]{1,0:T(8,128)(2,1)S(1)} %collective-permute-done), channel_id=1, source_target_pairs={{0,8},{4,12},{8,0},{12,4},{1,9},{5,13},{9,1},{13,5},{2,10},{6,14},... | collective-permute-start | bytes 589832 | tf_op jit(solution)/shard_map/ppermute | solution.py:287
  18.8 7.8 %collective-permute-start.11 = (bf16[256,384]{1,0:T(8,128)(2,1)S(1)}, bf16[256,384]{1,0:T(8,128)(2,1)S(1)}, u32[]{:S(2)}, u32[]{:S(2)}) collective-permute-start(bf16[256,384]{1,0:T(8,128)(2,1)S(1)} %collective-permute-done.10.near1), channel_id=1, source_target_pairs={{0,2},{2,0},{1,3},{3,1},{4,6},{6,4},{5,7},{7,5},{8,10},{10,8},{9,1... | collective-permute-start | bytes 589832 | tf_op jit(solution)/shard_map/ppermute | solution.py:290
  20.9 9.8 %collective-permute-start.6 = (bf16[256,384]{1,0:T(8,128)(2,1)S(1)}, bf16[256,384]{1,0:T(8,128)(2,1)S(1)}, u32[]{:S(2)}, u32[]{:S(2)}) collective-permute-start(bf16[256,384]{1,0:T(8,128)(2,1)S(1)} %collective-permute-done.1.near3), channel_id=1, source_target_pairs={{0,4},{4,0},{8,12},{12,8},{1,5},{5,1},{9,13},{13,9},{2,6},{6,2},{1... | collective-permute-start | bytes 589832 | tf_op jit(solution)/shard_map/ppermute | solution.py:287
  22.5 7.3 %collective-permute-start.4 = (bf16[256,384]{1,0:T(8,128)(2,1)S(1)}, bf16[256,384]{1,0:T(8,128)(2,1)S(1)}, u32[]{:S(2)}, u32[]{:S(2)}) collective-permute-start(bf16[256,384]{1,0:T(8,128)(2,1)S(1)} %collective-permute-done.1.near3), channel_id=1, source_target_pairs={{0,2},{2,0},{1,3},{3,1},{4,6},{6,4},{5,7},{7,5},{8,10},{10,8},{9,1... | collective-permute-start | bytes 589832 | tf_op jit(solution)/shard_map/ppermute | solution.py:290
  26.9 4.8 %collective-permute-start.14 = (bf16[256,768]{1,0:T(8,128)(2,1)S(1)}, bf16[256,768]{1,0:T(8,128)(2,1)S(1)}, u32[]{:S(2)}, u32[]{:S(2)}) collective-permute-start(bf16[256,768]{1,0:T(8,128)(2,1)S(1)} %fusion.2.own1), channel_id=1, source_target_pairs={{0,1},{1,0},{2,3},{3,2},{4,5},{5,4},{6,7},{7,6},{8,9},{9,8},{10,11... | collective-permute-start | bytes 1179656 | tf_op jit(solution)/shard_map/ppermute | solution.py:293
  27.0 4.6 %collective-permute-start.12 = (bf16[256,384]{1,0:T(8,128)(2,1)S(1)}, bf16[256,384]{1,0:T(8,128)(2,1)S(1)}, u32[]{:S(2)}, u32[]{:S(2)}) collective-permute-start(bf16[256,384]{1,0:T(8,128)(2,1)S(1)} %collective-permute-done.10.near1), channel_id=1, source_target_pairs={{0,1},{1,0},{2,3},{3,2},{4,5},{5,4},{6,7},{7,6},{8,9},{9,8},{10,11... | collective-permute-start | bytes 589832 | tf_op jit(solution)/shard_map/ppermute | solution.py:293
  28.5 3.2 %collective-permute-start.13 = (bf16[256,768]{1,0:T(8,128)(2,1)S(1)}, bf16[256,768]{1,0:T(8,128)(2,1)S(1)}, u32[]{:S(2)}, u32[]{:S(2)}) collective-permute-start(bf16[256,768]{1,0:T(8,128)(2,1)S(1)} %fusion.3.own0), channel_id=1, source_target_pairs={{0,1},{1,0},{2,3},{3,2},{4,5},{5,4},{6,7},{7,6},{8,9},{9,8},{10,11... | collective-permute-start | bytes 1179656 | tf_op jit(solution)/shard_map/ppermute | solution.py:293
  30.6 1.2 %copy-start.1 = (bf16[256,384]{1,0:T(8,128)(2,1)S(1)}, bf16[256,384]{1,0:T(8,128)(2,1)}, u32[]{:S(2)}) copy-start(bf16[256,384]{1,0:T(8,128)(2,1)} %near0.1) | copy-start | bytes 589828
  30.6 1.1 %copy-start.3 = (s32[24]{0:T(128)S(1)}, s32[24]{0:T(128)}, u32[]{:S(2)}) copy-start(s32[24]{0:T(128)} %get-tuple-element.18.places) | copy-start | bytes 292
  30.6 2.7 %collective-permute-start.9 = (bf16[256,768]{1,0:T(8,128)(2,1)S(1)}, bf16[256,768]{1,0:T(8,128)(2,1)S(1)}, u32[]{:S(2)}, u32[]{:S(2)}) collective-permute-start(bf16[256,768]{1,0:T(8,128)(2,1)S(1)} %fusion.4.own3), channel_id=1, source_target_pairs={{0,1},{1,0},{2,3},{3,2},{4,5},{5,4},{6,7},{7,6},{8,9},{9,8},{10,11... | collective-permute-start | bytes 1179656 | tf_op jit(solution)/shard_map/ppermute | solution.py:293
  31.1 2.2 %copy-start.2 = (f32[24,128]{1,0:T(8,128)S(1)}, f32[24,128]{1,0:T(8,128)}, u32[]{:S(2)}) copy-start(f32[24,128]{1,0:T(8,128)} %get-tuple-element.19.weights) | copy-start | bytes 36868
  31.1 2.2 %collective-permute-start.8 = (bf16[256,768]{1,0:T(8,128)(2,1)S(1)}, bf16[256,768]{1,0:T(8,128)(2,1)S(1)}, u32[]{:S(2)}, u32[]{:S(2)}) collective-permute-start(bf16[256,768]{1,0:T(8,128)(2,1)S(1)} %fusion.5.own2), channel_id=1, source_target_pairs={{0,1},{1,0},{2,3},{3,2},{4,5},{5,4},{6,7},{7,6},{8,9},{9,8},{10,11... | collective-permute-start | bytes 1179656 | tf_op jit(solution)/shard_map/ppermute | solution.py:293
  31.6 1.6 %collective-permute-start.5 = (bf16[256,384]{1,0:T(8,128)(2,1)S(1)}, bf16[256,384]{1,0:T(8,128)(2,1)S(1)}, u32[]{:S(2)}, u32[]{:S(2)}) collective-permute-start(bf16[256,384]{1,0:T(8,128)(2,1)S(1)} %collective-permute-done.1.near3), channel_id=1, source_target_pairs={{0,1},{1,0},{2,3},{3,2},{4,5},{5,4},{6,7},{7,6},{8,9},{9,8},{10,11... | collective-permute-start | bytes 589832 | tf_op jit(solution)/shard_map/ppermute | solution.py:293
  38.9 2.1 %collective-permute-start.15 = (bf16[384,768]{1,0:T(8,128)(2,1)S(1)}, bf16[384,768]{1,0:T(8,128)(2,1)S(1)}, u32[]{:S(2)}, u32[]{:S(2)}) collective-permute-start(bf16[384,768]{1,0:T(8,128)(2,1)S(1)} %get-tuple-element.29), channel_id=1, source_target_pairs={{0,1},{1,0},{2,3},{3,2},{4,5},{5,4},{6,7},{7,6},{8,9},{9,8},{10,11... | collective-permute-start | bytes 1769480 | tf_op jit(solution)/shard_map/ppermute | solution.py:293

commit v2 on v0

--- a/solution.py
+++ b/solution.py
@@ -251,7 +251,7 @@
         near[tile_at(row_tiles - 1), :] = jnp.zeros((TILE, near.shape[1]), near.dtype)
 
     col_tiles = jnp.maximum(2 * ((total + 1) // 2), 8)
-    for count, deep, columns in ((4, 2, (8, 10)), (6, 3, (10, 12, 14)), (8, 2, (14,))):
+    for count, deep, columns in ((4, 4, (8, 10)), (6, 3, (10, 12, 14)), (8, 4, (14,))):
         for tiles in columns:
 
             @pl.when(jnp.logical_and(col_tiles == tiles, row_tiles == count))

time: 42.4 us -> 43.2 us (1.019)
  Pallas kernels: 8.66 us -> 9.35 us
    pallas_call x1, Pallas kernels: 5.66 us -> 6.35 us  [gathered_body(): pl.pallas_call(pair_kernel, out_shape=buffers + (jax.ShapeDtypeStruct((sh...]
where the time goes in v2:
time: 43.2 us; the launch traced here: 42.9 us
  starting transfers between devices  15.9 us (37%)
  waiting for transfers between devices  9.53 us (22%)
  Pallas kernels  9.35 us (22%)
  matrix products  4.93 us (11%)
  other arithmetic  1.29 us (3%)
  local copies, waits for them, and re-layouts  1.1 us (3%)
  between operations  0.84 us (2%)
    ppermute x4, starting transfers between devices, across_z(): lax.ppermute(value, 'loop', [(i, i ^ step) for i in range(loop_size)])  8.53 us
    ppermute x4, waiting for transfers between devices, across_x(): return lax.ppermute(value, 'enc', [(0, 1), (1, 0)])  8.35 us
    pallas_call x1, Pallas kernels, gathered_body(): pl.pallas_call(pair_kernel, out_shape=buffers + (jax.ShapeDtypeStruct((sh...  6.35 us
    ppermute x4, starting transfers between devices, across_x(): return lax.ppermute(value, 'enc', [(0, 1), (1, 0)])  5.57 us
    dot_general x4, matrix products, features(): value = jnp.dot(near, head_weight, preferred_element_type=jnp.float32)  2.39 us
    ppermute x8, starting transfers between devices, across_cores(): return lax.ppermute(value, 'rep', [(0, 1), (1, 0)])  1.8 us
    pallas_call x1, Pallas kernels, gathered_body(): pl.pallas_call(pack_kernel, out_shape=buffers, in_specs=[smem] + [vmem] *...  1.53 us
    pallas_call x1, Pallas kernels, gathered_body(): pl.pallas_call(prep_kernel, out_shape=(jax.ShapeDtypeStruct((PLACES, TILE...  1.48 us
  transfers between devices with their start and end apart: 16, of which 6 were waited for; matrix products, arithmetic and copies ran while one was open for 12% of the time, Pallas kernels for 7%

profile of v2, /device:TPU:0, one launch (start us, length us, event | category | flops | bytes accessed | tf_op | source)
XLA Modules:
  0.0 42.9 jit_solution(13651051253919237529)
XLA Ops:
  0.6 0.0 copy-start
  0.6 1.1 %copy-done = bf16[384,768]{1,0:T(8,128)(2,1)S(1)} copy-done((bf16[384,768]{1,0:T(8,128)(2,1)S(1)}, bf16[384,768]{1,0:T(8,128)(2,1)}, u32[]{:S(2)}) %copy-start) | copy-done | bytes 589848
  1.7 3.0 %collective-permute-start.2 = (bf16[192,768]{1,0:T(8,128)(2,1)S(1)}, bf16[192,768]{1,0:T(8,128)(2,1)S(1)}, u32[]{:S(2)}, u32[]{:S(2)}) collective-permute-start(bf16[192,768]{1,0:T(8,128)(2,1)S(1)} %constant_dynamic-slice_fusion), channel_id=1, source_target_pairs={{0,2},{2,0},{1,3},{3,1},{4,6},{6,4},{5,7},{7,5},{8,10},{10,8},{9,1... | collective-permute-start | bytes 884744 | tf_op jit(solution)/shard_map/ppermute | solution.py:292
  4.7 1.6 %collective-permute-start.10 = (bf16[256,384]{1,0:T(8,128)(2,1)}, bf16[256,384]{1,0:T(8,128)(2,1)S(1)}, u32[]{:S(2)}, u32[]{:S(2)}) collective-permute-start(bf16[256,384]{1,0:T(8,128)(2,1)} %near0.1), channel_id=1, source_target_pairs={{0,4},{4,0},{8,12},{12,8},{1,5},{5,1},{9,13},{13,9},{2,6},{6,2},{1... | collective-permute-start | bytes 589832 | tf_op jit(solution)/shard_map/ppermute | solution.py:289
  6.3 2.5 %collective-permute-start.1 = (bf16[256,384]{1,0:T(8,128)(2,1)}, bf16[256,384]{1,0:T(8,128)(2,1)S(1)}, u32[]{:S(2)}, u32[]{:S(2)}) collective-permute-start(bf16[256,384]{1,0:T(8,128)(2,1)} %near0.1), channel_id=1, source_target_pairs={{0,12},{4,8},{8,4},{12,0},{1,13},{5,9},{9,5},{13,1},{2,14},{6,10},... | collective-permute-start | bytes 589832 | tf_op jit(solution)/shard_map/ppermute | solution.py:289
  8.8 0.5 %collective-permute-start = (bf16[256,384]{1,0:T(8,128)(2,1)}, bf16[256,384]{1,0:T(8,128)(2,1)S(1)}, u32[]{:S(2)}, u32[]{:S(2)}) collective-permute-start(bf16[256,384]{1,0:T(8,128)(2,1)} %near0.1), channel_id=1, source_target_pairs={{0,2},{2,0},{1,3},{3,1},{4,6},{6,4},{5,7},{7,5},{8,10},{10,8},{9,1... | collective-permute-start | bytes 589832 | tf_op jit(solution)/shard_map/ppermute | solution.py:292
  9.3 3.2 %collective-permute-done.2 = bf16[192,768]{1,0:T(8,128)(2,1)S(1)} collective-permute-done((bf16[192,768]{1,0:T(8,128)(2,1)S(1)}, bf16[192,768]{1,0:T(8,128)(2,1)S(1)}, u32[]{:S(2)}, u32[]{:S(2)}) %collective-permute-start.2) | collective-permute-done | bytes 294944 | tf_op jit(solution)/shard_map/ppermute | solution.py:292
  12.6 0.0 collective-permute-start.3
  12.6 1.3 %fusion.9 = f32[256,768]{1,0:T(8,128)S(1)} fusion(bf16[256,384]{1,0:T(8,128)(2,1)} %near0.1, bf16[384,768]{1,0:T(8,128)(2,1)S(1)} %copy-done), kind=kOutput, calls=%fused_computation.17 | convolution fusion | flops 150994944 | bytes 1572864 | tf_op jit(solution)/shard_map/dot_general | solution.py:331
  13.9 1.5 %shard_map.59 = (f32[24,128]{1,0:T(8,128)}, s32[24]{0:T(128)}) custom-call(s32[4]{0:T(128)} %counts_ref.1, f32[16,128]{1,0:T(8,128)} %bitcast.31), custom_call_target="tpu_custom_call" | custom-call | tf_op jit(solution)/shard_map/pallas_call | solution.py:302
  15.4 0.6 %collective-permute-done = bf16[256,384]{1,0:T(8,128)(2,1)S(1)} collective-permute-done((bf16[256,384]{1,0:T(8,128)(2,1)}, bf16[256,384]{1,0:T(8,128)(2,1)S(1)}, u32[]{:S(2)}, u32[]{:S(2)}) %collective-permute-start) | collective-permute-done | bytes 196640 | tf_op jit(solution)/shard_map/ppermute | solution.py:292
  15.9 2.8 %collective-permute-start.7 = (bf16[256,384]{1,0:T(8,128)(2,1)S(1)}, bf16[256,384]{1,0:T(8,128)(2,1)S(1)}, u32[]{:S(2)}, u32[]{:S(2)}) collective-permute-start(bf16[256,384]{1,0:T(8,128)(2,1)S(1)} %collective-permute-done), channel_id=1, source_target_pairs={{0,8},{4,12},{8,0},{12,4},{1,9},{5,13},{9,1},{13,5},{2,10},{6,14},... | collective-permute-start | bytes 589832 | tf_op jit(solution)/shard_map/ppermute | solution.py:289
  18.8 0.0 collective-permute-done.10.near1
  18.8 1.5 %collective-permute-start.11 = (bf16[256,384]{1,0:T(8,128)(2,1)S(1)}, bf16[256,384]{1,0:T(8,128)(2,1)S(1)}, u32[]{:S(2)}, u32[]{:S(2)}) collective-permute-start(bf16[256,384]{1,0:T(8,128)(2,1)S(1)} %collective-permute-done.10.near1), channel_id=1, source_target_pairs={{0,2},{2,0},{1,3},{3,1},{4,6},{6,4},{5,7},{7,5},{8,10},{10,8},{9,1... | collective-permute-start | bytes 589832 | tf_op jit(solution)/shard_map/ppermute | solution.py:292
  20.3 0.4 fusion.8
  20.6 0.0 collective-permute-done.3
  20.7 0.2 maximum_select_fusion
  20.8 0.0 collective-permute-done.1.near3
  20.9 1.6 %collective-permute-start.6 = (bf16[256,384]{1,0:T(8,128)(2,1)S(1)}, bf16[256,384]{1,0:T(8,128)(2,1)S(1)}, u32[]{:S(2)}, u32[]{:S(2)}) collective-permute-start(bf16[256,384]{1,0:T(8,128)(2,1)S(1)} %collective-permute-done.1.near3), channel_id=1, source_target_pairs={{0,4},{4,0},{8,12},{12,8},{1,5},{5,1},{9,13},{13,9},{2,6},{6,2},{1... | collective-permute-start | bytes 589832 | tf_op jit(solution)/shard_map/ppermute | solution.py:289
  22.5 0.5 %collective-permute-start.4 = (bf16[256,384]{1,0:T(8,128)(2,1)S(1)}, bf16[256,384]{1,0:T(8,128)(2,1)S(1)}, u32[]{:S(2)}, u32[]{:S(2)}) collective-permute-start(bf16[256,384]{1,0:T(8,128)(2,1)S(1)} %collective-permute-done.1.near3), channel_id=1, source_target_pairs={{0,2},{2,0},{1,3},{3,1},{4,6},{6,4},{5,7},{7,5},{8,10},{10,8},{9,1... | collective-permute-start | bytes 589832 | tf_op jit(solution)/shard_map/ppermute | solution.py:292
  23.0 3.5 %collective-permute-done.11 = bf16[256,384]{1,0:T(8,128)(2,1)S(1)} collective-permute-done((bf16[256,384]{1,0:T(8,128)(2,1)S(1)}, bf16[256,384]{1,0:T(8,128)(2,1)S(1)}, u32[]{:S(2)}, u32[]{:S(2)}) %collective-permute-start.11) | collective-permute-done | bytes 196640 | tf_op jit(solution)/shard_map/ppermute | solution.py:292
  26.6 0.4 fusion.2.own1
  26.9 0.1 collective-permute-start.14
  27.0 0.5 %collective-permute-start.12 = (bf16[256,384]{1,0:T(8,128)(2,1)S(1)}, bf16[256,384]{1,0:T(8,128)(2,1)S(1)}, u32[]{:S(2)}, u32[]{:S(2)}) collective-permute-start(bf16[256,384]{1,0:T(8,128)(2,1)S(1)} %collective-permute-done.10.near1), channel_id=1, source_target_pairs={{0,1},{1,0},{2,3},{3,2},{4,5},{5,4},{6,7},{7,6},{8,9},{9,8},{10,11... | collective-permute-start | bytes 589832 | tf_op jit(solution)/shard_map/ppermute | solution.py:295
  27.5 0.4 fusion.3.own0
  27.9 0.6 %collective-permute-done.7 = bf16[256,384]{1,0:T(8,128)(2,1)S(1)} collective-permute-done((bf16[256,384]{1,0:T(8,128)(2,1)S(1)}, bf16[256,384]{1,0:T(8,128)(2,1)S(1)}, u32[]{:S(2)}, u32[]{:S(2)}) %collective-permute-start.7) | collective-permute-done | bytes 196640 | tf_op jit(solution)/shard_map/ppermute | solution.py:289
  28.5 0.0 collective-permute-start.13
  28.5 0.4 fusion.7
  28.8 1.0 %collective-permute-done.4 = bf16[256,384]{1,0:T(8,128)(2,1)S(1)} collective-permute-done((bf16[256,384]{1,0:T(8,128)(2,1)S(1)}, bf16[256,384]{1,0:T(8,128)(2,1)S(1)}, u32[]{:S(2)}, u32[]{:S(2)}) %collective-permute-start.4) | collective-permute-done | bytes 196640 | tf_op jit(solution)/shard_map/ppermute | solution.py:292
  29.8 0.4 fusion.6
  30.2 0.4 fusion.4.own3
  30.6 0.0 copy-start.1
  30.6 0.0 copy-start.3
  30.6 0.1 collective-permute-start.9
  30.7 0.4 fusion.5.own2
  31.1 0.0 copy-start.2
  31.1 0.6 %collective-permute-start.8 = (bf16[256,768]{1,0:T(8,128)(2,1)S(1)}, bf16[256,768]{1,0:T(8,128)(2,1)S(1)}, u32[]{:S(2)}, u32[]{:S(2)}) collective-permute-start(bf16[256,768]{1,0:T(8,128)(2,1)S(1)} %fusion.5.own2), channel_id=1, source_target_pairs={{0,1},{1,0},{2,3},{3,2},{4,5},{5,4},{6,7},{7,6},{8,9},{9,8},{10,11... | collective-permute-start | bytes 1179656 | tf_op jit(solution)/shard_map/ppermute | solution.py:295
  31.6 0.0 collective-permute-done.12.lent1
  31.6 0.1 collective-permute-start.5
  31.7 0.0 collective-permute-done.14.other1
  31.7 0.0 collective-permute-done.13.other0
  31.7 1.5 %shard_map.60 = (bf16[2304,768]{1,0:T(8,128)(2,1)S(1)}, f32[24,128]{1,0:T(8,128)S(1)}, bf16[1536,384]{1,0:T(8,128)(2,1)S(1)}) custom-call(s32[24]{0:T(128)S(1)} %copy-done.3, bf16[256,384]{1,0:T(8,128)(2,1)S(1)} %copy-done.1, bf16[256,384]{1,0:T(8,128)(2,1)S(1)} %collective-permute-done.10.near1, bf16[256,384]{1,0:T(8,128)(2,1)S(1)} %collective-permute-done.6.near2, ...), custom_call_target="tpu_custom_call" | custom-call | tf_op jit(solution)/shard_map/pallas_call | solution.py:346
  33.3 0.0 collective-permute-done.9.other3
  33.3 6.3 %shard_map.61 = (bf16[2304,768]{1,0:T(8,128)(2,1)S(1)}, f32[24,128]{1,0:T(8,128)S(1)}, bf16[1536,384]{1,0:T(8,128)(2,1)S(1)}, bf16[256,768]{1,0:T(8,128)(2,1)S(1...) custom-call(s32[24]{0:T(128)S(1)} %copy-done.3, ...), custom_call_target="tpu_custom_call", output_to_operand_aliasing={{0}: (5, {}), {1}: (6, {}), {2}: (7, {})} | custom-call | tf_op jit(solution)/shard_map/pallas_call | solution.py:367
  39.7 0.5 %collective-permute-start.15 = (bf16[384,768]{1,0:T(8,128)(2,1)S(1)}, bf16[384,768]{1,0:T(8,128)(2,1)S(1)}, u32[]{:S(2)}, u32[]{:S(2)}) collective-permute-start(bf16[384,768]{1,0:T(8,128)(2,1)S(1)} %get-tuple-element.31), channel_id=1, source_target_pairs={{0,1},{1,0},{2,3},{3,2},{4,5},{5,4},{6,7},{7,6},{8,9},{9,8},{10,11... | collective-permute-start | bytes 1769480 | tf_op jit(solution)/shard_map/ppermute | solution.py:295
  40.2 1.1 %convolution_convert_fusion = bf16[256,384]{1,0:T(8,128)(2,1)} fusion(bf16[256,768]{1,0:T(8,128)(2,1)S(1)} %get-tuple-element.29, bf16[384,768]{1,0:T(8,128)(2,1)S(1)} %copy-done), kind=kOutput, calls=%fused_computation.11 | convolution fusion | flops 151093248 | bytes 1179648 | tf_op jit(solution)/shard_map/dot_general | solution.py:382
  41.3 0.6 %collective-permute-done.15 = bf16[384,768]{1,0:T(8,128)(2,1)S(1)} collective-permute-done((bf16[384,768]{1,0:T(8,128)(2,1)S(1)}, bf16[384,768]{1,0:T(8,128)(2,1)S(1)}, u32[]{:S(2)}, u32[]{:S(2)}) %collective-permute-start.15) | collective-permute-done | bytes 589856 | tf_op jit(solution)/shard_map/ppermute | solution.py:295
  41.8 1.1 %convert_add_fusion = f32[384,768]{1,0:T(8,128)} fusion(f32[384,768]{1,0:T(8,128)S(1)} %get-tuple-element.30, bf16[384,768]{1,0:T(8,128)(2,1)S(1)} %collective-permute-done.15), kind=kLoop, calls=%fused_computation.10 | loop fusion | flops 589824 | bytes 2949120 | tf_op jit(solution)/shard_map/add | solution.py:385
  (7 shorter events, 0.0 us)
Async XLA Ops:
  0.6 1.1 %copy-start = (bf16[384,768]{1,0:T(8,128)(2,1)S(1)}, bf16[384,768]{1,0:T(8,128)(2,1)}, u32[]{:S(2)}) copy-start(bf16[384,768]{1,0:T(8,128)(2,1)} %param.5) | copy-start | bytes 1769476
  1.7 10.8 %collective-permute-start.2 = (bf16[192,768]{1,0:T(8,128)(2,1)S(1)}, bf16[192,768]{1,0:T(8,128)(2,1)S(1)}, u32[]{:S(2)}, u32[]{:S(2)}) collective-permute-start(bf16[192,768]{1,0:T(8,128)(2,1)S(1)} %constant_dynamic-slice_fusion), channel_id=1, source_target_pairs={{0,2},{2,0},{1,3},{3,1},{4,6},{6,4},{5,7},{7,5},{8,10},{10,8},{9,1... | collective-permute-start | bytes 884744 | tf_op jit(solution)/shard_map/ppermute | solution.py:292
  4.7 14.1 %collective-permute-start.10 = (bf16[256,384]{1,0:T(8,128)(2,1)}, bf16[256,384]{1,0:T(8,128)(2,1)S(1)}, u32[]{:S(2)}, u32[]{:S(2)}) collective-permute-start(bf16[256,384]{1,0:T(8,128)(2,1)} %near0.1), channel_id=1, source_target_pairs={{0,4},{4,0},{8,12},{12,8},{1,5},{5,1},{9,13},{13,9},{2,6},{6,2},{1... | collective-permute-start | bytes 589832 | tf_op jit(solution)/shard_map/ppermute | solution.py:289
  6.3 14.5 %collective-permute-start.1 = (bf16[256,384]{1,0:T(8,128)(2,1)}, bf16[256,384]{1,0:T(8,128)(2,1)S(1)}, u32[]{:S(2)}, u32[]{:S(2)}) collective-permute-start(bf16[256,384]{1,0:T(8,128)(2,1)} %near0.1), channel_id=1, source_target_pairs={{0,12},{4,8},{8,4},{12,0},{1,13},{5,9},{9,5},{13,1},{2,14},{6,10},... | collective-permute-start | bytes 589832 | tf_op jit(solution)/shard_map/ppermute | solution.py:289
  8.8 7.2 %collective-permute-start = (bf16[256,384]{1,0:T(8,128)(2,1)}, bf16[256,384]{1,0:T(8,128)(2,1)S(1)}, u32[]{:S(2)}, u32[]{:S(2)}) collective-permute-start(bf16[256,384]{1,0:T(8,128)(2,1)} %near0.1), channel_id=1, source_target_pairs={{0,2},{2,0},{1,3},{3,1},{4,6},{6,4},{5,7},{7,5},{8,10},{10,8},{9,1... | collective-permute-start | bytes 589832 | tf_op jit(solution)/shard_map/ppermute | solution.py:292
  12.6 8.1 %collective-permute-start.3 = (bf16[192,768]{1,0:T(8,128)(2,1)S(1)}, bf16[192,768]{1,0:T(8,128)(2,1)S(1)}, u32[]{:S(2)}, u32[]{:S(2)}) collective-permute-start(bf16[192,768]{1,0:T(8,128)(2,1)S(1)} %collective-permute-done.2), channel_id=1, source_target_pairs={{0,1},{1,0},{2,3},{3,2},{4,5},{5,4},{6,7},{7,6},{8,9},{9,8},{10,11... | collective-permute-start | bytes 884744 | tf_op jit(solution)/shard_map/ppermute | solution.py:295
  15.9 12.5 %collective-permute-start.7 = (bf16[256,384]{1,0:T(8,128)(2,1)S(1)}, bf16[256,384]{1,0:T(8,128)(2,1)S(1)}, u32[]{:S(2)}, u32[]{:S(2)}) collective-permute-start(bf16[256,384]{1,0:T(8,128)(2,1)S(1)} %collective-permute-done), channel_id=1, source_target_pairs={{0,8},{4,12},{8,0},{12,4},{1,9},{5,13},{9,1},{13,5},{2,10},{6,14},... | collective-permute-start | bytes 589832 | tf_op jit(solution)/shard_map/ppermute | solution.py:289
  18.8 7.8 %collective-permute-start.11 = (bf16[256,384]{1,0:T(8,128)(2,1)S(1)}, bf16[256,384]{1,0:T(8,128)(2,1)S(1)}, u32[]{:S(2)}, u32[]{:S(2)}) collective-permute-start(bf16[256,384]{1,0:T(8,128)(2,1)S(1)} %collective-permute-done.10.near1), channel_id=1, source_target_pairs={{0,2},{2,0},{1,3},{3,1},{4,6},{6,4},{5,7},{7,5},{8,10},{10,8},{9,1... | collective-permute-start | bytes 589832 | tf_op jit(solution)/shard_map/ppermute | solution.py:292
  20.9 9.8 %collective-permute-start.6 = (bf16[256,384]{1,0:T(8,128)(2,1)S(1)}, bf16[256,384]{1,0:T(8,128)(2,1)S(1)}, u32[]{:S(2)}, u32[]{:S(2)}) collective-permute-start(bf16[256,384]{1,0:T(8,128)(2,1)S(1)} %collective-permute-done.1.near3), channel_id=1, source_target_pairs={{0,4},{4,0},{8,12},{12,8},{1,5},{5,1},{9,13},{13,9},{2,6},{6,2},{1... | collective-permute-start | bytes 589832 | tf_op jit(solution)/shard_map/ppermute | solution.py:289
  22.5 7.3 %collective-permute-start.4 = (bf16[256,384]{1,0:T(8,128)(2,1)S(1)}, bf16[256,384]{1,0:T(8,128)(2,1)S(1)}, u32[]{:S(2)}, u32[]{:S(2)}) collective-permute-start(bf16[256,384]{1,0:T(8,128)(2,1)S(1)} %collective-permute-done.1.near3), channel_id=1, source_target_pairs={{0,2},{2,0},{1,3},{3,1},{4,6},{6,4},{5,7},{7,5},{8,10},{10,8},{9,1... | collective-permute-start | bytes 589832 | tf_op jit(solution)/shard_map/ppermute | solution.py:292
  26.9 4.8 %collective-permute-start.14 = (bf16[256,768]{1,0:T(8,128)(2,1)S(1)}, bf16[256,768]{1,0:T(8,128)(2,1)S(1)}, u32[]{:S(2)}, u32[]{:S(2)}) collective-permute-start(bf16[256,768]{1,0:T(8,128)(2,1)S(1)} %fusion.2.own1), channel_id=1, source_target_pairs={{0,1},{1,0},{2,3},{3,2},{4,5},{5,4},{6,7},{7,6},{8,9},{9,8},{10,11... | collective-permute-start | bytes 1179656 | tf_op jit(solution)/shard_map/ppermute | solution.py:295
  27.0 4.6 %collective-permute-start.12 = (bf16[256,384]{1,0:T(8,128)(2,1)S(1)}, bf16[256,384]{1,0:T(8,128)(2,1)S(1)}, u32[]{:S(2)}, u32[]{:S(2)}) collective-permute-start(bf16[256,384]{1,0:T(8,128)(2,1)S(1)} %collective-permute-done.10.near1), channel_id=1, source_target_pairs={{0,1},{1,0},{2,3},{3,2},{4,5},{5,4},{6,7},{7,6},{8,9},{9,8},{10,11... | collective-permute-start | bytes 589832 | tf_op jit(solution)/shard_map/ppermute | solution.py:295
  28.5 3.3 %collective-permute-start.13 = (bf16[256,768]{1,0:T(8,128)(2,1)S(1)}, bf16[256,768]{1,0:T(8,128)(2,1)S(1)}, u32[]{:S(2)}, u32[]{:S(2)}) collective-permute-start(bf16[256,768]{1,0:T(8,128)(2,1)S(1)} %fusion.3.own0), channel_id=1, source_target_pairs={{0,1},{1,0},{2,3},{3,2},{4,5},{5,4},{6,7},{7,6},{8,9},{9,8},{10,11... | collective-permute-start | bytes 1179656 | tf_op jit(solution)/shard_map/ppermute | solution.py:295
  30.6 1.2 %copy-start.1 = (bf16[256,384]{1,0:T(8,128)(2,1)S(1)}, bf16[256,384]{1,0:T(8,128)(2,1)}, u32[]{:S(2)}) copy-start(bf16[256,384]{1,0:T(8,128)(2,1)} %near0.1) | copy-start | bytes 589828
  30.6 1.1 %copy-start.3 = (s32[24]{0:T(128)S(1)}, s32[24]{0:T(128)}, u32[]{:S(2)}) copy-start(s32[24]{0:T(128)} %get-tuple-element.19.places) | copy-start | bytes 292
  30.6 2.7 %collective-permute-start.9 = (bf16[256,768]{1,0:T(8,128)(2,1)S(1)}, bf16[256,768]{1,0:T(8,128)(2,1)S(1)}, u32[]{:S(2)}, u32[]{:S(2)}) collective-permute-start(bf16[256,768]{1,0:T(8,128)(2,1)S(1)} %fusion.4.own3), channel_id=1, source_target_pairs={{0,1},{1,0},{2,3},{3,2},{4,5},{5,4},{6,7},{7,6},{8,9},{9,8},{10,11... | collective-permute-start | bytes 1179656 | tf_op jit(solution)/shard_map/ppermute | solution.py:295
  31.1 2.2 %copy-start.2 = (f32[24,128]{1,0:T(8,128)S(1)}, f32[24,128]{1,0:T(8,128)}, u32[]{:S(2)}) copy-start(f32[24,128]{1,0:T(8,128)} %get-tuple-element.20.weights) | copy-start | bytes 36868
  31.1 2.2 %collective-permute-start.8 = (bf16[256,768]{1,0:T(8,128)(2,1)S(1)}, bf16[256,768]{1,0:T(8,128)(2,1)S(1)}, u32[]{:S(2)}, u32[]{:S(2)}) collective-permute-start(bf16[256,768]{1,0:T(8,128)(2,1)S(1)} %fusion.5.own2), channel_id=1, source_target_pairs={{0,1},{1,0},{2,3},{3,2},{4,5},{5,4},{6,7},{7,6},{8,9},{9,8},{10,11... | collective-permute-start | bytes 1179656 | tf_op jit(solution)/shard_map/ppermute | solution.py:295
  31.6 1.6 %collective-permute-start.5 = (bf16[256,384]{1,0:T(8,128)(2,1)S(1)}, bf16[256,384]{1,0:T(8,128)(2,1)S(1)}, u32[]{:S(2)}, u32[]{:S(2)}) collective-permute-start(bf16[256,384]{1,0:T(8,128)(2,1)S(1)} %collective-permute-done.1.near3), channel_id=1, source_target_pairs={{0,1},{1,0},{2,3},{3,2},{4,5},{5,4},{6,7},{7,6},{8,9},{9,8},{10,11... | collective-permute-start | bytes 589832 | tf_op jit(solution)/shard_map/ppermute | solution.py:295
  39.7 2.1 %collective-permute-start.15 = (bf16[384,768]{1,0:T(8,128)(2,1)S(1)}, bf16[384,768]{1,0:T(8,128)(2,1)S(1)}, u32[]{:S(2)}, u32[]{:S(2)}) collective-permute-start(bf16[384,768]{1,0:T(8,128)(2,1)S(1)} %get-tuple-element.31), channel_id=1, source_target_pairs={{0,1},{1,0},{2,3},{3,2},{4,5},{5,4},{6,7},{7,6},{8,9},{9,8},{10,11... | collective-permute-start | bytes 1769480 | tf_op jit(solution)/shard_map/ppermute | solution.py:295
